TPU v7x, 32 devices: a whole 2x2x4 slice. The times are simulated.
32 devices in a mesh: gx: 8 (over z, x), gy: 4 (over y, core).
Axes of the slice: x: 2, y: 2, z: 4, core: 2. Of those that a mesh axis runs over, the one named last changes fastest.
Arguments:
- anchors: float32 [3, 1024], P(None, ('gx', 'gy')), may hold values from 0 to 1
- directions: float32 [3, 1024], P(None, ('gx', 'gy')), may hold values from -1 to 1
- ray_start: float32 [1024], P(('gx', 'gy')), may hold values from 0 to 1
- camera_ids: int32 [1024], P(('gx', 'gy')), may hold values from 0 to 255
- brick_ids: int32 [1024, 4], P(('gx', 'gy')), may hold values from 0 to 31, all different within a row; in each aligned block of 32 rows (0 to 31, 32 to 63, ...) at most 8 rows name the same one
- brick_rank: int32 [1024, 4], P(('gx', 'gy')), may hold values from 0 to 3, each once within a row
- targets: float32 [1024, 128], P(('gx', 'gy')), may hold values from -6 to 6
- planes: float32 [32, 12288, 128], P(('gx', 'gy')), may hold values from -6 to 6
- first_weight: float32 [32, 128, 256], P(('gx', 'gy')), may hold values from -0.5 to 0.5
- hidden_weight: float32 [32, 1, 256, 256], P(('gx', 'gy')), may hold values from -0.375 to 0.375
- feature_weight: float32 [32, 256, 128], P(('gx', 'gy')), may hold values from -0.375 to 0.375
- density_weight: float32 [32, 256], P(('gx', 'gy')), may hold values from -0.375 to 0.375
- poses: float32 [6, 256], replicated, may hold values from -0.1 to 0.1
Outputs:
- ray_feature: float32 [1024, 128], P(('gx', 'gy'))
- plane_grad: float32 [32, 12288, 128], P(('gx', 'gy'))
- first_grad: float32 [32, 128, 256], P(('gx', 'gy'))
- hidden_grad: float32 [32, 1, 256, 256], P(('gx', 'gy'))
- feature_grad: float32 [32, 256, 128], P(('gx', 'gy'))
- density_grad: float32 [32, 256], P(('gx', 'gy'))
- pose_grad: float32 [6, 256], replicated
Inputs may be any that keep to these rules, and one draw needn't show every extreme that they name: `brick_ids`: each ray names 4 different bricks; among the rays of one device no brick is named more than 8 times, and in every draw some device's rays name some brick exactly 8 times. `brick_rank`: each row holds every number of 0 to 3 once.
All inputs are finite; a program needn't handle non-finite values.
Results may differ from a plain program's by a relative error of at most 0.014.
Values sent between devices are 32-bit elements; how exact they have to be, the bound alone decides.
A program may use at most 256 MiB of HBM per device.

v0:
```python
import jax
import jax.numpy as jnp
from jax import lax
from jax.sharding import PartitionSpec as P

K = 4
S = 4
P_SIZE = 64


sample_step = 0.125
plane_pairs = ((0, 1), (0, 2), (1, 2))


def smooth_weight(fraction):
    return fraction * fraction * (3.0 - 2.0 * fraction)


def axis_weights(coord, cells):
    scaled = coord * P_SIZE
    floor_c = jnp.floor(scaled)
    weight = smooth_weight(scaled - floor_c)[:, None]
    low_c = jnp.mod(floor_c.astype(jnp.int32), P_SIZE)
    high_c = jnp.mod(low_c + 1, P_SIZE)
    low_hit = (cells[None, :] == low_c[:, None]).astype(jnp.float32)
    high_hit = (cells[None, :] == high_c[:, None]).astype(jnp.float32)
    return (1.0 - weight) * low_hit + weight * high_hit


def lookup_block(planes_flat, points):
    count = points.shape[1]
    cells = jnp.arange(P_SIZE)
    summed = jnp.zeros((count, planes_flat.shape[1]), jnp.float32)
    for plane_index, coord_pair in enumerate(plane_pairs):
        row_factor = axis_weights(points[coord_pair[0]], cells)
        col_factor = axis_weights(points[coord_pair[1]], cells)
        table = (row_factor[:, :, None] * col_factor[:, None, :]).reshape(count, P_SIZE * P_SIZE)
        plane_rows = planes_flat[
            plane_index * P_SIZE * P_SIZE : (plane_index + 1) * P_SIZE * P_SIZE
        ]
        summed = summed + jnp.dot(
            table, plane_rows, precision=lax.Precision.HIGHEST, preferred_element_type=jnp.float32
        )
    return summed


def lookup(planes_flat, points):
    count = points.shape[1]
    block = min(512, count)
    blocks = count // block
    grouped = points.reshape(3, blocks, block).transpose(1, 0, 2)

    def one_block(piece):
        return lookup_block(planes_flat, piece)

    return lax.map(one_block, grouped).reshape(count, planes_flat.shape[1])


def brick_samples(
    planes_flat, first_weight, hidden_weight, feature_weight, density_weight, received
):
    sources, slot_total, flat_width = received.shape
    points = received.reshape(sources * slot_total, 3, S).transpose(1, 0, 2).reshape(3, -1)
    features = lookup(planes_flat, points).astype(jnp.bfloat16)
    hidden = jax.nn.silu(
        jnp.dot(features, first_weight.astype(jnp.bfloat16), preferred_element_type=jnp.float32)
    ).astype(jnp.bfloat16)
    hidden = jax.nn.silu(
        jnp.dot(hidden, hidden_weight[0].astype(jnp.bfloat16), preferred_element_type=jnp.float32)
    ).astype(jnp.bfloat16)
    colors = jnp.tanh(
        jnp.dot(hidden, feature_weight.astype(jnp.bfloat16), preferred_element_type=jnp.float32)
    )
    density = jax.nn.softplus(
        jnp.dot(hidden, density_weight.astype(jnp.bfloat16), preferred_element_type=jnp.float32)
    )
    return (colors.reshape(sources, slot_total, -1), density.reshape(sources, slot_total, S))


def composite(density, colors):
    optical_depth = density * sample_step
    before = jnp.cumsum(optical_depth, axis=-1) - optical_depth
    weight = jnp.exp(-before) * (1.0 - jnp.exp(-optical_depth))
    feature = jnp.sum(weight[..., None] * colors, axis=-2)
    passing = jnp.exp(-jnp.sum(optical_depth, axis=-1))
    return (feature, passing)


def pick_brick():
    return brick_samples


def ray_composite(segment_feature, segment_pass, brick_rank):
    transmit = jnp.ones(segment_pass.shape, segment_pass.dtype)
    for other_seg in range(K):
        in_front = brick_rank[:, other_seg][:, None] < brick_rank
        transmit = transmit * jnp.where(in_front, segment_pass[:, other_seg][:, None], 1.0)
    return jnp.sum(transmit[:, :, None] * segment_feature, axis=1)


def cross_rows(left, right):
    return jnp.stack(
        [
            left[1] * right[2] - left[2] * right[1],
            left[2] * right[0] - left[0] * right[2],
            left[0] * right[1] - left[1] * right[0],
        ]
    )


def sample_points(anchors, directions, ray_start, ray_pose, brick_rank):
    rotation = ray_pose[0:3]
    offset = ray_pose[3:6]
    moved_anchor = anchors + cross_rows(rotation, anchors) + offset
    moved_direction = directions + cross_rows(rotation, directions)
    place_along = (
        brick_rank.astype(jnp.float32)[:, :, None] * S + jnp.arange(S)[None, None, :] + 0.5
    )
    distance = ray_start[:, None, None] + place_along * sample_step
    return moved_anchor[:, :, None, None] + distance[None] * moved_direction[:, :, None, None]


def slot_numbers(target_brick, brick_count):
    onehot = (target_brick[:, None] == jnp.arange(brick_count)[None, :]).astype(jnp.float32)
    rows = target_brick.shape[0]
    lower = (jnp.arange(rows)[:, None] > jnp.arange(rows)[None, :]).astype(jnp.float32)
    before = jnp.dot(
        lower, onehot, precision=lax.Precision.HIGHEST, preferred_element_type=jnp.float32
    )
    return jnp.sum(before * onehot, axis=1).astype(jnp.int32)


def to_slots(route, rows):
    return lax.dot_general(
        route,
        rows,
        (((0,), (0,)), ((), ())),
        precision=lax.Precision.HIGHEST,
        preferred_element_type=jnp.float32,
    )


def from_slots(route, rows):
    return jnp.dot(route, rows, precision=lax.Precision.HIGHEST, preferred_element_type=jnp.float32)


def per_device(
    anchors,
    directions,
    ray_start,
    camera_ids,
    brick_ids,
    brick_rank,
    targets,
    planes,
    first_weight,
    hidden_weight,
    feature_weight,
    density_weight,
    poses,
):
    brick_count = lax.axis_size(("gx", "gy"))
    ray_count = anchors.shape[1]
    capacity = 2 * ray_count * K // brick_count
    selector = (jnp.arange(poses.shape[1])[:, None] == camera_ids[None, :]).astype(jnp.float32)

    def place(pose_table):
        ray_pose = jnp.dot(pose_table, selector, precision=lax.Precision.HIGHEST)
        return sample_points(anchors, directions, ray_start, ray_pose, brick_rank)

    points, pose_pullback = jax.vjp(place, poses)
    payload = points.transpose(1, 2, 0, 3).reshape(ray_count * K, 3 * S)
    target_brick = brick_ids.reshape(-1)
    flat_slot = target_brick * capacity + slot_numbers(target_brick, brick_count)
    route = (flat_slot[:, None] == jnp.arange(brick_count * capacity)[None, :]).astype(jnp.float32)
    outgoing = to_slots(route, payload).reshape(brick_count, capacity, 3 * S)
    params = (planes[0], first_weight[0], hidden_weight[0], feature_weight[0], density_weight[0])
    brick_fn = pick_brick()
    received = lax.all_to_all(outgoing, ("gx", "gy"), split_axis=0, concat_axis=0, tiled=True)
    values_out, optical_out = brick_fn(
        params[0], params[1], params[2], params[3], params[4], received
    )
    values_sent, optical_sent, received = (values_out, optical_out, received)
    values_home, optical_home = (
        lax.all_to_all(values_sent, ("gx", "gy"), split_axis=0, concat_axis=0, tiled=True),
        lax.all_to_all(optical_sent, ("gx", "gy"), split_axis=0, concat_axis=0, tiled=True),
    )
    segment_values = from_slots(route, values_home.reshape(brick_count * capacity, -1))
    segment_optical = from_slots(route, optical_home.reshape(brick_count * capacity, -1))

    def ray_from(values_part, optical_part):
        segment_feature, segment_pass = composite(
            optical_part.reshape(ray_count, K, S), values_part.reshape(ray_count, K, S, -1)
        )
        return ray_composite(segment_feature, segment_pass, brick_rank)

    ray_feature, ray_pullback = jax.vjp(ray_from, segment_values, segment_optical)
    values_grad, optical_grad = ray_pullback(ray_feature - targets)
    values_back = to_slots(route, values_grad).reshape(values_sent.shape)
    optical_back = to_slots(route, optical_grad).reshape(optical_sent.shape)
    values_cot, optical_cot = (
        lax.all_to_all(values_back, ("gx", "gy"), split_axis=0, concat_axis=0, tiled=True),
        lax.all_to_all(optical_back, ("gx", "gy"), split_axis=0, concat_axis=0, tiled=True),
    )
    outputs_unused, brick_pullback = jax.vjp(
        brick_fn, params[0], params[1], params[2], params[3], params[4], received
    )
    gradients = brick_pullback((values_cot, optical_cot))
    point_home = lax.all_to_all(gradients[5], ("gx", "gy"), split_axis=0, concat_axis=0, tiled=True)
    point_rows = from_slots(route, point_home.reshape(brick_count * capacity, 3 * S))
    point_grad = point_rows.reshape(ray_count, K, 3, S).transpose(2, 0, 1, 3)
    pose_local = pose_pullback(point_grad)[0]
    pose_grad = lax.psum(pose_local, ("gx", "gy"))
    return (
        ray_feature,
        gradients[0][None],
        gradients[1][None],
        gradients[2][None],
        gradients[3][None],
        gradients[4][None],
        pose_grad,
    )


def solution(mesh):
    in_specs = (
        P(None, ("gx", "gy")),
        P(None, ("gx", "gy")),
        P(("gx", "gy")),
        P(("gx", "gy")),
        P(("gx", "gy"), None),
        P(("gx", "gy"), None),
        P(("gx", "gy"), None),
        P(("gx", "gy"), None, None),
        P(("gx", "gy"), None, None),
        P(("gx", "gy"), None, None, None),
        P(("gx", "gy"), None, None),
        P(("gx", "gy"), None),
        P(),
    )
    out_specs = (
        P(("gx", "gy"), None),
        P(("gx", "gy"), None, None),
        P(("gx", "gy"), None, None),
        P(("gx", "gy"), None, None, None),
        P(("gx", "gy"), None, None),
        P(("gx", "gy"), None),
        P(),
    )
    return jax.shard_map(
        per_device, mesh=mesh, in_specs=in_specs, out_specs=out_specs, check_vma=False
    )
```

profile of v0, /device:TPU:0, one launch (start us, length us, event | category | flops | bytes accessed | tf_op | source)
XLA Modules:
  0.0 640.4 jit_solution(16024808857223118782)
XLA Ops:
  25.8 135.1 %while.108 = (s32[]{:T(128)}, bf16[2,512,128]{2,1,0:T(8,128)(2,1)S(1)}, f32[2,3,512]{2,1,0:T(4,128)S(1)}, f32[12288,128]{1,0:T(8,128)}, s32[]{:T(128)}, /*index=5*/s32[]{:T(128)}, s32[]{}, s32[]{}) while((s32[]{:T(128)}, bf16[2,512,128]{2,1,0:T(8,128)(2,1)S(1)}, f32[2,3,512]{2,1,0:T(4,128)S(1)}, f32[12288,128]{1,0:T(8,128)}, s32[]{:T(128)}, ...), condition=%wide.region_2.3_spmd, body=%wide.region_1.2_spmd.sunk | while | flops 9670641664 | bytes 117514952 | solution.py:56
  49.5 9.4 %broadcast_multiply_fusion.10 = (f32[512,64,64]{0,2,1:T(8,128)}, f32[512,64,64]{0,2,1:T(8,128)}, f32[512,64,64]{0,2,1:T(8,128)}) fusion(f32[512,64]{0,1:T(8,128)S(1)} %get-tuple-element.2838, f32[512,64]{0,1:T(8,128)S(1)} %select_add_fusion.13, f32[512,64]{0,1:T(8,128)S(1)} %get-tuple-element.2844), kind=kLoop, calls=%fused_computation.3.clone.1 | loop fusion | flops 6291456 | bytes 25559040 | tf_op jit(solution)/shard_map/while/body/eval_jaxpr/mul | solution.py:37
  59.0 16.0 %fusion.281 = f32[512,128]{1,0:T(8,128)S(1)} fusion(f32[512,4096]{0,1:T(8,128)} %bitcast.421, f32[12288,128]{1,0:T(8,128)} %get-tuple-element.2989), kind=kOutput, calls=%fused_computation.4.clone.1 | convolution fusion | flops 3221225472 | bytes 10747904 | tf_op jit(solution)/shard_map/while/body/eval_jaxpr/dot_general | solution.py:41
  75.0 15.1 %fusion.282 = f32[512,128]{1,0:T(8,128)S(1)} fusion(f32[512,4096]{0,1:T(8,128)S(1)} %bitcast.420, f32[12288,128]{1,0:T(8,128)} %get-tuple-element.2989), kind=kOutput, calls=%fused_computation.6.clone.1 | convolution fusion | flops 3221225472 | bytes 10747904 | tf_op jit(solution)/shard_map/while/body/eval_jaxpr/dot_general | solution.py:41
  90.1 15.0 %fusion.283 = bf16[2,512,128]{2,1,0:T(8,128)(2,1)S(1)} fusion(bf16[2,512,128]{2,1,0:T(8,128)(2,1)S(1)} %get-tuple-element.2979, s32[]{:T(128)} %get-tuple-element.2978, f32[512,128]{1,0:T(8,128)S(1)} %fusion.281, f32[512,128]{1,0:T(8,128)S(1)} %fusion.282, f32[512,4096]{0,1:T(8,128)S(1)} %bitcast.419, f32[12288,128]{1,0:T(8,128)} %get-tuple-element.2989), kind=kOutput, calls=%fused_computation.13.clone.1 | convolution fusion | flops 3221356544 | bytes 11272704 | tf_op jit(solution)/shard_map/while/body/eval_jaxpr/dot_general | solution.py:41
  105.4 9.4 %broadcast_multiply_fusion.10 = (f32[512,64,64]{0,2,1:T(8,128)}, f32[512,64,64]{0,2,1:T(8,128)}, f32[512,64,64]{0,2,1:T(8,128)}) fusion(f32[512,64]{0,1:T(8,128)S(1)} %get-tuple-element.2838, f32[512,64]{0,1:T(8,128)S(1)} %select_add_fusion.13, f32[512,64]{0,1:T(8,128)S(1)} %get-tuple-element.2844), kind=kLoop, calls=%fused_computation.3.clone.1 | loop fusion | flops 6291456 | bytes 25559040 | tf_op jit(solution)/shard_map/while/body/eval_jaxpr/mul | solution.py:37
  114.8 16.0 %fusion.281 = f32[512,128]{1,0:T(8,128)S(1)} fusion(f32[512,4096]{0,1:T(8,128)} %bitcast.421, f32[12288,128]{1,0:T(8,128)} %get-tuple-element.2989), kind=kOutput, calls=%fused_computation.4.clone.1 | convolution fusion | flops 3221225472 | bytes 10747904 | tf_op jit(solution)/shard_map/while/body/eval_jaxpr/dot_general | solution.py:41
  130.8 15.1 %fusion.282 = f32[512,128]{1,0:T(8,128)S(1)} fusion(f32[512,4096]{0,1:T(8,128)S(1)} %bitcast.420, f32[12288,128]{1,0:T(8,128)} %get-tuple-element.2989), kind=kOutput, calls=%fused_computation.6.clone.1 | convolution fusion | flops 3221225472 | bytes 10747904 | tf_op jit(solution)/shard_map/while/body/eval_jaxpr/dot_general | solution.py:41
  145.9 15.0 %fusion.283 = bf16[2,512,128]{2,1,0:T(8,128)(2,1)S(1)} fusion(bf16[2,512,128]{2,1,0:T(8,128)(2,1)S(1)} %get-tuple-element.2979, s32[]{:T(128)} %get-tuple-element.2978, f32[512,128]{1,0:T(8,128)S(1)} %fusion.281, f32[512,128]{1,0:T(8,128)S(1)} %fusion.282, f32[512,4096]{0,1:T(8,128)S(1)} %bitcast.419, f32[12288,128]{1,0:T(8,128)} %get-tuple-element.2989), kind=kOutput, calls=%fused_computation.13.clone.1 | convolution fusion | flops 3221356544 | bytes 11272704 | tf_op jit(solution)/shard_map/while/body/eval_jaxpr/dot_general | solution.py:41
  169.1 181.5 %while.109 = (s32[]{:T(128)}, bf16[2,512,128]{2,1,0:T(8,128)(2,1)S(1)}, f32[2,512]{1,0:T(2,128)S(1)}, f32[2,512]{1,0:T(2,128)S(1)}, f32[2,512]{1,0:T(2,128)S(1)}...) while((s32[]{:T(128)}, ...), condition=%wide.region_15.16_spmd.clone.clone, body=%wide.region_14.15_spmd.clone.clone.sunk | while | flops 9671700480 | bytes 198627264 | solution.py:56
  172.6 9.4 %broadcast_multiply_fusion.11 = (f32[512,64,64]{0,2,1:T(8,128)}, f32[512,64,64]{0,2,1:T(8,128)}, f32[512,64,64]{0,2,1:T(8,128)}) fusion(f32[512,64]{0,1:T(8,128)S(1)} %select_add_fusion.14, f32[512,64]{0,1:T(8,128)S(1)} %select_add_fusion.15, f32[512,64]{0,1:T(8,128)S(1)} %select_add_fusion.16), kind=kLoop, calls=%fused_computation.62.clone.1 | loop fusion | flops 6291456 | bytes 25559040 | tf_op jit(solution)/shard_map/jvp()/while/body/eval_jaxpr/mul | solution.py:37
  182.0 13.0 %constant_dynamic-update-slice_fusion.22 = (f32[2,512,4096]{1,2,0:T(8,128)}, f32[2,512,4096]{1,2,0:T(8,128)}) fusion(f32[2,512,4096]{1,2,0:T(8,128)} %get-tuple-element.3049, f32[1,512,4096]{1,2,0:T(8,128)} %bitcast.407, s32[]{:T(128)} %get-tuple-element.3026, f32[2,512,4096]{1,2,0:T(8,128)} %get-tuple-element.3047, f32[1,512,4096]{1,2,0:T(8,128)} %bitcast.411), kind=kLoop, calls=%fused_computation.106.clone.1 | loop fusion | bytes 33554944 | tf_op jit(solution)/shard_map/jvp()/while/body/jit(dynamic_update_index_in_dim)/dynamic_update_slice | solution.py:56
  200.3 15.5 %fusion.291 = f32[512,128]{1,0:T(8,128)S(1)} fusion(f32[512,4096]{0,1:T(8,128)S(1)} %bitcast.416, f32[4096,128]{1,0:T(8,128)} %get-tuple-element.3083), kind=kOutput, calls=%fused_computation.444.clone.1 | convolution fusion | flops 3221225472 | bytes 10747904 | tf_op jit(solution)/shard_map/jvp()/while/body/eval_jaxpr/dot_general | solution.py:41
  215.9 15.4 %convolution_add_fusion.3 = f32[512,128]{1,0:T(8,128)S(1)} fusion(f32[512,128]{1,0:T(8,128)S(1)} %fusion.291, f32[512,4096]{0,1:T(8,128)S(1)} %bitcast.414, f32[4096,128]{1,0:T(8,128)} %get-tuple-element.3084), kind=kOutput, calls=%fused_computation.68.clone.1 | convolution fusion | flops 3221291008 | bytes 11010048 | tf_op jit(solution)/shard_map/jvp()/while/body/eval_jaxpr/dot_general | solution.py:41
  231.3 15.2 %fusion.292 = bf16[2,512,128]{2,1,0:T(8,128)(2,1)S(1)} fusion(bf16[2,512,128]{2,1,0:T(8,128)(2,1)S(1)} %get-tuple-element.3027, s32[]{:T(128)} %get-tuple-element.3026, f32[512,128]{1,0:T(8,128)S(1)} %convolution_add_fusion.3, f32[512,4096]{0,1:T(8,128)S(1)} %bitcast.410, f32[4096,128]{1,0:T(8,128)} %get-tuple-element.3085), kind=kOutput, calls=%fused_computation.67.clone.1 | convolution fusion | flops 3221291008 | bytes 11010052 | tf_op jit(solution)/shard_map/jvp()/while/body/eval_jaxpr/dot_general | solution.py:41
  259.0 9.4 %broadcast_multiply_fusion.11 = (f32[512,64,64]{0,2,1:T(8,128)}, f32[512,64,64]{0,2,1:T(8,128)}, f32[512,64,64]{0,2,1:T(8,128)}) fusion(f32[512,64]{0,1:T(8,128)S(1)} %select_add_fusion.14, f32[512,64]{0,1:T(8,128)S(1)} %select_add_fusion.15, f32[512,64]{0,1:T(8,128)S(1)} %select_add_fusion.16), kind=kLoop, calls=%fused_computation.62.clone.1 | loop fusion | flops 6291456 | bytes 25559040 | tf_op jit(solution)/shard_map/jvp()/while/body/eval_jaxpr/mul | solution.py:37
  268.4 13.2 %constant_dynamic-update-slice_fusion.22 = (f32[2,512,4096]{1,2,0:T(8,128)}, f32[2,512,4096]{1,2,0:T(8,128)}) fusion(f32[2,512,4096]{1,2,0:T(8,128)} %get-tuple-element.3049, f32[1,512,4096]{1,2,0:T(8,128)} %bitcast.407, s32[]{:T(128)} %get-tuple-element.3026, f32[2,512,4096]{1,2,0:T(8,128)} %get-tuple-element.3047, f32[1,512,4096]{1,2,0:T(8,128)} %bitcast.411), kind=kLoop, calls=%fused_computation.106.clone.1 | loop fusion | bytes 33554944 | tf_op jit(solution)/shard_map/jvp()/while/body/jit(dynamic_update_index_in_dim)/dynamic_update_slice | solution.py:56
  287.0 15.3 %fusion.291 = f32[512,128]{1,0:T(8,128)S(1)} fusion(f32[512,4096]{0,1:T(8,128)S(1)} %bitcast.416, f32[4096,128]{1,0:T(8,128)} %get-tuple-element.3083), kind=kOutput, calls=%fused_computation.444.clone.1 | convolution fusion | flops 3221225472 | bytes 10747904 | tf_op jit(solution)/shard_map/jvp()/while/body/eval_jaxpr/dot_general | solution.py:41
  302.3 15.4 %convolution_add_fusion.3 = f32[512,128]{1,0:T(8,128)S(1)} fusion(f32[512,128]{1,0:T(8,128)S(1)} %fusion.291, f32[512,4096]{0,1:T(8,128)S(1)} %bitcast.414, f32[4096,128]{1,0:T(8,128)} %get-tuple-element.3084), kind=kOutput, calls=%fused_computation.68.clone.1 | convolution fusion | flops 3221291008 | bytes 11010048 | tf_op jit(solution)/shard_map/jvp()/while/body/eval_jaxpr/dot_general | solution.py:41
  317.8 15.3 %fusion.292 = bf16[2,512,128]{2,1,0:T(8,128)(2,1)S(1)} fusion(bf16[2,512,128]{2,1,0:T(8,128)(2,1)S(1)} %get-tuple-element.3027, s32[]{:T(128)} %get-tuple-element.3026, f32[512,128]{1,0:T(8,128)S(1)} %convolution_add_fusion.3, f32[512,4096]{0,1:T(8,128)S(1)} %bitcast.410, f32[4096,128]{1,0:T(8,128)} %get-tuple-element.3085), kind=kOutput, calls=%fused_computation.67.clone.1 | convolution fusion | flops 3221291008 | bytes 11010052 | tf_op jit(solution)/shard_map/jvp()/while/body/eval_jaxpr/dot_general | solution.py:41
  360.4 14.1 %all-to-all-done.2 = f32[32,8,512]{2,1,0:T(8,128)S(1)} async-done(((f32[32,8,512]{2,1,0:T(8,128)}), f32[32,8,512]{2,1,0:T(8,128)S(1)}, u32[]{:S(2)}, u32[]{:S(2)}) %all-to-all-start.2) | async-done | bytes 524320 | tf_op jit(solution)/shard_map/all_to_all | solution.py:185
  394.2 12.6 %all-to-all-done.4 = f32[32,8,512]{2,1,0:T(8,128)S(1)} async-done(((f32[32,8,512]{2,1,0:T(8,128)}), f32[32,8,512]{2,1,0:T(8,128)S(1)}, u32[]{:S(2)}, u32[]{:S(2)}) %all-to-all-start.4) | async-done | bytes 524320 | tf_op jit(solution)/shard_map/all_to_all | solution.py:202
  413.2 174.9 %while.110 = (s32[]{:T(128)}, f32[12288,128]{1,0:T(8,128)}, f32[2,3,512]{2,1,0:T(4,128)S(1)}, f32[2,512,4096]{1,2,0:T(8,128)}, f32[2,512,128]{2,1,0:T(8,128)S(1)...) while((s32[]{:T(128)}, f32[12288,128]{1,0:T(8,128)}, ...), condition=%wide.region_35.36_spmd.clone, body=%wide.region_16.35_spmd.clone.sunk | while | flops 19359428608 | bytes 96335152 | solution.py:56
  457.6 13.7 %multiply_reduce_fusion.12 = (f32[512,64]{0,1:T(8,128)S(1)}, f32[512,64]{0,1:T(8,128)S(1)}, f32[512,64]{0,1:T(8,128)S(1)}, f32[512,64]{0,1:T(8,128)S(1)}, f32[512,64]{0,1:T(8,128)S(1)}, /*index=5*/f32[512,64]{0,1:T(8,128)S(1)}) fusion(f32[512,64]{0,1:T(8,128)S(1)} %bitcast.424, f32[512,64]{0,1:T(8,128)S(1)} %dynamic-slice_bitcast_fusion.4, ...), kind=kOutput, calls=%fused_computation.177.clone.1 | convolution fusion | flops 3246194688 | bytes 20447236 | tf_op jit(solution)/shard_map/transpose(jvp())/while/body/eval_jaxpr/dot_general | solution.py:41
  483.1 10.1 %fusion.314 = f32[4096,128]{1,0:T(8,128)} fusion(f32[2,512,4096]{1,2,0:T(8,128)} %get-tuple-element.3157, s32[]{:T(128)S(6)} %sub.691, f32[2,512,128]{2,1,0:T(8,128)S(1)} %get-tuple-element.3156), kind=kOutput, calls=%fused_computation.168.clone.1 | convolution fusion | flops 3221225472 | bytes 10748928 | tf_op jit(solution)/shard_map/transpose(jvp())/while/body/eval_jaxpr/dot_general | solution.py:41
  493.3 10.1 %fusion.315 = f32[4096,128]{1,0:T(8,128)} fusion(f32[2,512,4096]{1,2,0:T(8,128)} %get-tuple-element.3155, s32[]{:T(128)S(6)} %sub.691, f32[2,512,128]{2,1,0:T(8,128)S(1)} %get-tuple-element.3156), kind=kOutput, calls=%fused_computation.170.clone.1 | convolution fusion | flops 3221225472 | bytes 10748928 | tf_op jit(solution)/shard_map/transpose(jvp())/while/body/eval_jaxpr/dot_general | solution.py:41
  532.9 13.7 %multiply_reduce_fusion.12 = (f32[512,64]{0,1:T(8,128)S(1)}, f32[512,64]{0,1:T(8,128)S(1)}, f32[512,64]{0,1:T(8,128)S(1)}, f32[512,64]{0,1:T(8,128)S(1)}, f32[512,64]{0,1:T(8,128)S(1)}, /*index=5*/f32[512,64]{0,1:T(8,128)S(1)}) fusion(f32[512,64]{0,1:T(8,128)S(1)} %bitcast.424, f32[512,64]{0,1:T(8,128)S(1)} %dynamic-slice_bitcast_fusion.4, ...), kind=kOutput, calls=%fused_computation.177.clone.1 | convolution fusion | flops 3246194688 | bytes 20447236 | tf_op jit(solution)/shard_map/transpose(jvp())/while/body/eval_jaxpr/dot_general | solution.py:41
  549.1 9.3 %fusion.313 = f32[4096,128]{1,0:T(8,128)S(1)} fusion(f32[2,512,4096]{1,2,0:T(8,128)} %get-tuple-element.3158, s32[]{:T(128)S(6)} %sub.691, f32[2,512,128]{2,1,0:T(8,128)S(1)} %get-tuple-element.3156), kind=kOutput, calls=%fused_computation.166.clone.1 | convolution fusion | flops 3221225472 | bytes 10748928 | tf_op jit(solution)/shard_map/transpose(jvp())/while/body/eval_jaxpr/dot_general | solution.py:41
  558.4 10.1 %fusion.314 = f32[4096,128]{1,0:T(8,128)} fusion(f32[2,512,4096]{1,2,0:T(8,128)} %get-tuple-element.3157, s32[]{:T(128)S(6)} %sub.691, f32[2,512,128]{2,1,0:T(8,128)S(1)} %get-tuple-element.3156), kind=kOutput, calls=%fused_computation.168.clone.1 | convolution fusion | flops 3221225472 | bytes 10748928 | tf_op jit(solution)/shard_map/transpose(jvp())/while/body/eval_jaxpr/dot_general | solution.py:41
  568.5 10.1 %fusion.315 = f32[4096,128]{1,0:T(8,128)} fusion(f32[2,512,4096]{1,2,0:T(8,128)} %get-tuple-element.3155, s32[]{:T(128)S(6)} %sub.691, f32[2,512,128]{2,1,0:T(8,128)S(1)} %get-tuple-element.3156), kind=kOutput, calls=%fused_computation.170.clone.1 | convolution fusion | flops 3221225472 | bytes 10748928 | tf_op jit(solution)/shard_map/transpose(jvp())/while/body/eval_jaxpr/dot_general | solution.py:41
  578.6 9.4 %fusion.316 = f32[12288,128]{1,0:T(8,128)} fusion(f32[12288,128]{1,0:T(8,128)} %get-tuple-element.3122, f32[4096,128]{1,0:T(8,128)S(1)} %fusion.313, f32[4096,128]{1,0:T(8,128)} %fusion.314, f32[4096,128]{1,0:T(8,128)} %fusion.315, pred[]{:T(512)S(6)} %compare.42), kind=kLoop, calls=%fused_computation.183.clone.1 | loop fusion | flops 6291456 | bytes 18874368 | tf_op jit(solution)/shard_map/transpose(jvp())/while/body/eval_jaxpr/add_any | solution.py:38
  601.5 38.4 %psum.7 = f32[6,256]{1,0:T(8,128)} all-reduce(f32[6,256]{1,0:T(8,128)S(1)} %fusion.126), channel_id=1, replica_groups=mesh['gx'=8,'gy'=4] {'gx','gy'}, use_global_device_ids=true, to_apply=%region_38.39 | all-reduce | flops 1536 | bytes 12288 | tf_op jit(solution)/shard_map/psum | solution.py:213
  (374 shorter events, 181.5 us)
Async XLA Ops:
  8.2 16.6 %all-to-all-start = ((f32[32,8,12]{2,1,0:T(8,128)}), f32[32,8,12]{2,1,0:T(8,128)S(1)}, u32[]{:S(2)}, u32[]{:S(2)}) async-start(f32[32,8,12]{2,1,0:T(8,128)} %fusion.120), calls=%async_computation | async-start | bytes 262144 | tf_op jit(solution)/shard_map/all_to_all | solution.py:179
  25.8 135.2 %copy-start.10 = (f32[1,128,256]{2,1,0:T(8,128)S(1)}, f32[1,128,256]{2,1,0:T(8,128)}, u32[]{:S(2)}) copy-start(f32[1,128,256]{2,1,0:T(8,128)} %param.27) | copy-start | bytes 393220
  25.8 135.2 %copy-start.31 = (f32[1,1,256,256]{3,2,1,0:T(8,128)S(1)}, f32[1,1,256,256]{3,2,1,0:T(8,128)}, u32[]{:S(2)}) copy-start(f32[1,1,256,256]{3,2,1,0:T(8,128)} %param.28) | copy-start | bytes 786436
  59.0 31.1 %slice-start.4 = ((s8[8388608]{0:T(1024)(128)(4,1)}), s8[4194304]{0:T(1024)(128)(4,1)S(1)}, s32[]{:S(2)}) async-start(s8[8388608]{0:T(1024)(128)(4,1)} %bitcast.417), calls=%async_computation.10 | async-start | bytes 8388608 | tf_op jit(solution)/shard_map/while
  114.8 31.1 %slice-start.4 = ((s8[8388608]{0:T(1024)(128)(4,1)}), s8[4194304]{0:T(1024)(128)(4,1)S(1)}, s32[]{:S(2)}) async-start(s8[8388608]{0:T(1024)(128)(4,1)} %bitcast.417), calls=%async_computation.10 | async-start | bytes 8388608 | tf_op jit(solution)/shard_map/while
  163.0 190.2 %all-to-all-start.1 = ((f32[32,8,4]{1,2,0:T(4,128)}), f32[32,8,4]{1,2,0:T(4,128)}, u32[]{:S(2)}, u32[]{:S(2)}) async-start(f32[32,8,4]{1,2,0:T(4,128)} %copy.91), calls=%async_computation.1 | async-start | bytes 131072 | tf_op jit(solution)/shard_map/all_to_all | solution.py:186
  169.0 181.6 %copy-start.11 = (f32[1,128,256]{2,1,0:T(8,128)S(1)}, f32[1,128,256]{2,1,0:T(8,128)}, u32[]{:S(2)}) copy-start(f32[1,128,256]{2,1,0:T(8,128)} %param.27) | copy-start | bytes 393220
  169.0 181.9 %copy-start.9 = (f32[1,256,128]{2,1,0:T(8,128)S(1)}, f32[1,256,128]{2,1,0:T(8,128)}, u32[]{:S(2)}) copy-start(f32[1,256,128]{2,1,0:T(8,128)} %param.29) | copy-start | bytes 393220
  169.0 190.9 %copy-start.21 = (s32[32,4]{0,1:T(4,128)S(1)}, s32[32,4]{0,1:T(4,128)}, u32[]{:S(2)}) copy-start(s32[32,4]{0,1:T(4,128)} %multiply_add_fusion.3) | copy-start | bytes 1540
  169.0 191.3 %copy-start.17 = (s32[32,4]{0,1:T(4,128)S(1)}, s32[32,4]{0,1:T(4,128)}, u32[]{:S(2)}) copy-start(s32[32,4]{0,1:T(4,128)} %param.24) | copy-start | bytes 1540
  169.0 191.3 %copy-start.25 = (s32[32]{0:T(128)S(1)}, s32[32]{0:T(128)}, u32[]{:S(2)}) copy-start(s32[32]{0:T(128)} %get-tuple-element.2417) | copy-start | bytes 388
  169.0 191.3 %copy-start.26 = (s32[32]{0:T(128)S(1)}, s32[32]{0:T(128)}, u32[]{:S(2)}) copy-start(s32[32]{0:T(128)} %get-tuple-element.2418) | copy-start | bytes 388
  169.1 191.3 %copy-start.27 = (s32[32]{0:T(128)S(1)}, s32[32]{0:T(128)}, u32[]{:S(2)}) copy-start(s32[32]{0:T(128)} %get-tuple-element.2419) | copy-start | bytes 388
  169.1 191.3 %copy-start.28 = (s32[32]{0:T(128)S(1)}, s32[32]{0:T(128)}, u32[]{:S(2)}) copy-start(s32[32]{0:T(128)} %get-tuple-element.2420) | copy-start | bytes 388
  169.1 206.7 %copy-start.18 = (f32[32,128]{1,0:T(8,128)S(1)}, f32[32,128]{1,0:T(8,128)}, u32[]{:S(2)}) copy-start(f32[32,128]{1,0:T(8,128)} %param.25) | copy-start | bytes 49156
  169.1 207.4 %copy-start.13 = (s32[32,8]{1,0:T(8,128)S(1)}, s32[32,8]{1,0:T(8,128)}, u32[]{:S(2)}) copy-start(s32[32,8]{1,0:T(8,128)} %copy-done.12) | copy-start | bytes 3076
  169.1 207.4 %copy-start.30 = (s32[128]{0:T(128)S(1)}, s32[128]{0:T(128)}, u32[]{:S(2)}) copy-start(s32[128]{0:T(128)} %copy-done.29) | copy-start | bytes 1540
  350.6 42.2 %copy-start.4 = (bf16[2,512,128]{2,1,0:T(8,128)(2,1)}, bf16[2,512,128]{2,1,0:T(8,128)(2,1)S(1)}, u32[]{:S(2)}) copy-start(bf16[2,512,128]{2,1,0:T(8,128)(2,1)S(1)} %get-tuple-element.1686) | copy-start | bytes 786436
  350.6 40.7 %copy-start.32 = (f32[1,1,256,256]{3,2,1,0:T(8,128)S(1)}, f32[1,1,256,256]{3,2,1,0:T(8,128)}, u32[]{:S(2)}) copy-start(f32[1,1,256,256]{3,2,1,0:T(8,128)} %param.28) | copy-start | bytes 786436
  353.1 39.7 %copy-start.24 = (f32[1,256]{1,0:T(1,128)S(1)}, f32[1,256]{1,0:T(1,128)}, u32[]{:S(2)}) copy-start(f32[1,256]{1,0:T(1,128)} %param.30) | copy-start | bytes 3076
  353.1 21.3 %all-to-all-start.2 = ((f32[32,8,512]{2,1,0:T(8,128)}), f32[32,8,512]{2,1,0:T(8,128)S(1)}, u32[]{:S(2)}, u32[]{:S(2)}) async-start(f32[32,8,512]{2,1,0:T(8,128)} %reshape.2830), calls=%async_computation.2 | async-start | bytes 1048576 | tf_op jit(solution)/shard_map/all_to_all | solution.py:185
  378.2 10.5 %all-to-all-start.3 = ((f32[32,8,4]{1,2,0:T(4,128)}), f32[32,8,4]{1,2,0:T(4,128)S(1)}, u32[]{:S(2)}, u32[]{:S(2)}) async-start(f32[32,8,4]{1,2,0:T(4,128)} %fusion.118), calls=%async_computation.3 | async-start | bytes 131072 | tf_op jit(solution)/shard_map/all_to_all | solution.py:203
  388.7 18.2 %all-to-all-start.4 = ((f32[32,8,512]{2,1,0:T(8,128)}), f32[32,8,512]{2,1,0:T(8,128)S(1)}, u32[]{:S(2)}, u32[]{:S(2)}) async-start(f32[32,8,512]{2,1,0:T(8,128)} %fusion.116), calls=%async_computation.4 | async-start | bytes 1048576 | tf_op jit(solution)/shard_map/all_to_all | solution.py:202
  413.1 179.6 %copy-start.5 = (bf16[2,512,128]{2,1,0:T(8,128)(2,1)S(1)}, bf16[2,512,128]{2,1,0:T(8,128)(2,1)}, u32[]{:S(2)}) copy-start(bf16[2,512,128]{2,1,0:T(8,128)(2,1)} %copy-done.4) | copy-start | bytes 786436
  413.1 179.6 %copy-start.7 = (bf16[1024,256]{1,0:T(8,128)(2,1)S(1)}, bf16[1024,256]{1,0:T(8,128)(2,1)}, u32[]{:S(2)}) copy-start(bf16[1024,256]{1,0:T(8,128)(2,1)} %copy-done.6) | copy-start | bytes 1572868
  413.1 187.9 %copy-start.16 = (f32[32,4,4]{0,2,1:T(4,128)S(1)}, f32[32,4,4]{0,2,1:T(4,128)}, u32[]{:S(2)}) copy-start(f32[32,4,4]{0,2,1:T(4,128)} %copy-done.15) | copy-start | bytes 6148
  413.1 187.8 %copy-start.22 = (s32[32,4]{0,1:T(4,128)S(1)}, s32[32,4]{0,1:T(4,128)}, u32[]{:S(2)}) copy-start(s32[32,4]{0,1:T(4,128)} %multiply_add_fusion.3) | copy-start | bytes 1540
  413.1 188.2 %copy-start.19 = (f32[3,32]{1,0:T(4,128)S(1)}, f32[3,32]{1,0:T(4,128)}, u32[]{:S(2)}) copy-start(f32[3,32]{1,0:T(4,128)} %param.20) | copy-start | bytes 1156
  413.1 188.2 %copy-start.20 = (f32[3,32]{1,0:T(4,128)S(1)}, f32[3,32]{1,0:T(4,128)}, u32[]{:S(2)}) copy-start(f32[3,32]{1,0:T(4,128)} %param.19) | copy-start | bytes 1156
  413.2 188.2 %copy-start.33 = (s32[32]{0:T(128)S(1)}, s32[32]{0:T(128)}, u32[]{:S(2)}) copy-start(s32[32]{0:T(128)} %param.22) | copy-start | bytes 388
  588.0 51.9 %copy-start.1 = (f32[6,256]{1,0:T(8,128)S(1)}, f32[6,256]{1,0:T(8,128)}, u32[]{:S(2)}) copy-start(f32[6,256]{1,0:T(8,128)} %param.31) | copy-start | bytes 18436
  589.7 11.2 %all-to-all-start.5 = ((f32[32,8,12]{2,1,0:T(8,128)}), f32[32,8,12]{2,1,0:T(8,128)S(1)}, u32[]{:S(2)}, u32[]{:S(2)}) async-start(f32[32,8,12]{2,1,0:T(8,128)} %copy.113), calls=%async_computation.5 | async-start | bytes 262144 | tf_op jit(solution)/shard_map/all_to_all | solution.py:209
  (23 other events, 352.8 us)
where the time goes:
time: 644 us; the launch traced here: 640 us
  matrix products  323 us (50%)
  other arithmetic  83.6 us (13%)
  local copies, waits for them, and re-layouts  69 us (11%)
  loops' own time  57 us (9%)
  waiting for transfers between devices  39.9 us (6%)
  blocking collectives  38.4 us (6%)
  starting transfers between devices  27.7 us (4%)
    dot_general x24, matrix products, lookup_block(): jnp.dot(table, plane_rows, precision=lax.Precision.HIGHEST, preferred_ele...  305 us
    another operation x3, loops' own time, lookup(): return lax.map(one_block, grouped).reshape(count, planes_flat.shape[1])  57 us
    dynamic_update_slice x46, local copies, waits for them, and re-layouts, lookup(): return lax.map(one_block, grouped).reshape(count, planes_flat.shape[1])  43.6 us
    psum x1, blocking collectives, per_device(): pose_grad = lax.psum(pose_local, ('gx', 'gy'))  38.4 us
    mul x4, other arithmetic, lookup_block(): row_factor[:, :, None] * col_factor[:, None, :]  37.7 us
    add_any x2, other arithmetic, lookup_block(): planes_flat[plane_index * P_SIZE * P_SIZE:(plane_index + 1) * P_SIZE * P_...  17.8 us
    all_to_all x1, waiting for transfers between devices, per_device(): lax.all_to_all(values_sent, ('gx', 'gy'), split_axis=0, concat_axis=0, ti...  14.1 us
  transfers between devices with their start and end apart: 6, of which 4 were waited for; matrix products, arithmetic and copies ran while one was open for 29% of the time, Pallas kernels for 0%

commit v1 on v0

v1 whole, which is shorter than its diff:
```python
import functools

import jax
import jax.numpy as jnp
from jax import lax
from jax.experimental import pallas as pl
from jax.experimental.pallas import tpu as pltpu
from jax.sharding import PartitionSpec as P

SIDE = 64
STEP = 0.125
WIDTH = 128
AXES = ("gx", "gy")
BF16 = jnp.bfloat16
F32 = jnp.float32
MESH_ID = pl.DeviceIdType.MESH
VMEM_BYTES = 56 * 1024 * 1024


def dot(left, right, left_dim=1, right_dim=0, precision=None):
    return lax.dot_general(
        left,
        right,
        (((left_dim,), (right_dim,)), ((), ())),
        precision=precision,
        preferred_element_type=F32,
    )


def exact_dot(left, right, left_dim=1, right_dim=0):
    return dot(left, right, left_dim, right_dim, lax.Precision.HIGHEST)


def peer_id(index):
    side = lax.axis_size("gy")
    return (index // side, index % side)


def my_index():
    return lax.axis_index("gx") * lax.axis_size("gy") + lax.axis_index("gy")


def enter(count):
    me = my_index()
    barrier = pltpu.get_barrier_semaphore()

    def greet(step, carry):
        pl.semaphore_signal(
            barrier, inc=1, device_id=peer_id((me + step) % count), device_id_type=MESH_ID
        )
        return carry

    lax.fori_loop(1, count, greet, 0)
    pl.semaphore_wait(barrier, count - 1)


def rows_of(ref, index, rows):
    return ref.at[pl.ds(pl.multiple_of(index * rows, 8), rows)]


def remote_copy(count, step, source, target, rows, send_sem, recv_sem, shared):
    me = my_index()
    peer = (me + step) % count
    return pltpu.make_async_remote_copy(
        src_ref=source if shared else rows_of(source, peer, rows),
        dst_ref=rows_of(target, me, rows),
        send_sem=send_sem.at[step],
        recv_sem=recv_sem.at[me],
        device_id=peer_id(peer),
        device_id_type=MESH_ID,
    )


def send_all(count, source, target, rows, send_sem, recv_sem, shared=False):
    def send(step, carry):
        remote_copy(count, step, source, target, rows, send_sem, recv_sem, shared).start()
        return carry

    lax.fori_loop(1, count, send, 0)


def wait_all(count, source, target, rows, send_sem, recv_sem, shared=False):
    me = my_index()

    def arrive(step, carry):
        origin = (me + count - step) % count
        pltpu.make_async_remote_copy(
            src_ref=source if shared else rows_of(source, origin, rows),
            dst_ref=rows_of(target, origin, rows),
            send_sem=send_sem.at[step],
            recv_sem=recv_sem.at[origin],
            device_id=peer_id(origin),
            device_id_type=MESH_ID,
        ).wait_recv()
        return carry

    lax.fori_loop(1, count, arrive, 0)

    def leave(step, carry):
        remote_copy(count, step, source, target, rows, send_sem, recv_sem, shared).wait_send()
        return carry

    lax.fori_loop(1, count, leave, 0)


def keep_own(source, target, rows):
    here = pl.ds(pl.multiple_of(my_index() * rows, 8), rows)
    target[here, :] = source[here, :]


def points_kernel(count, rows, sent, received, landed, send_sem, recv_sem):
    enter(count)
    send_all(count, sent, landed, rows, send_sem, recv_sem)
    keep_own(sent, landed, rows)
    wait_all(count, sent, landed, rows, send_sem, recv_sem)
    received[...] = landed[...]


def owner_kernel(
    count,
    rows,
    ray_count,
    segs,
    sent,
    route,
    route_back,
    ranks,
    targets,
    ray_out,
    received,
    home,
    outgoing,
    landed,
    send_sem,
    recv_sem,
    send_sem2,
    recv_sem2,
):
    enter(count)
    send_all(count, sent, home, rows, send_sem, recv_sem)
    keep_own(sent, home, rows)
    wait_all(count, sent, home, rows, send_sem, recv_sem)
    listed = exact_dot(route[...], home[...])
    feature = [listed[k * ray_count : (k + 1) * ray_count, :WIDTH] for k in range(segs)]
    passing = [listed[k * ray_count : (k + 1) * ray_count, WIDTH:] for k in range(segs)]
    rank = [
        jnp.broadcast_to(ranks[:, k : k + 1], (ray_count, WIDTH)).astype(F32)
        for k in range(segs)
    ]

    def through(k, skipped):
        product = jnp.ones((ray_count, WIDTH), F32)
        for other in range(segs):
            if other != k and other != skipped:
                product = product * jnp.where(rank[other] < rank[k], passing[other], 1.0)
        return product

    transmit = [through(k, k) for k in range(segs)]
    ray = transmit[0] * feature[0]
    for k in range(1, segs):
        ray = ray + transmit[k] * feature[k]
    ray_out[...] = ray
    residual = ray - targets[...]
    along = [jnp.sum(residual * feature[k], axis=1, keepdims=True) for k in range(segs)]
    back = []
    for k in range(segs):
        pass_grad = jnp.zeros((ray_count, WIDTH), F32)
        for behind in range(segs):
            if behind != k:
                pass_grad = pass_grad + jnp.where(
                    rank[k] < rank[behind], through(behind, k) * along[behind], 0.0
                )
        back.append(jnp.concatenate([transmit[k] * residual, pass_grad], axis=1))
    outgoing[...] = exact_dot(route_back[...], jnp.concatenate(back, axis=0))
    send_all(count, outgoing, landed, rows, send_sem2, recv_sem2)
    keep_own(outgoing, landed, rows)
    wait_all(count, outgoing, landed, rows, send_sem2, recv_sem2)
    received[...] = landed[...]


def pose_kernel(count, rows, own, total, landed, send_sem, recv_sem):
    enter(count)
    send_all(count, own, landed, rows, send_sem, recv_sem, shared=True)
    here = pl.ds(pl.multiple_of(my_index() * rows, 8), rows)
    landed[here, :] = own[...]
    wait_all(count, own, landed, rows, send_sem, recv_sem, shared=True)
    summed = landed[0:rows, :]
    for index in range(1, count):
        summed = summed + landed[index * rows : (index + 1) * rows, :]
    total[...] = summed


def coordinate_rows(payload, samples):
    columns = payload.T
    return [
        jnp.concatenate([columns[c * samples + s : c * samples + s + 1] for s in range(samples)], 1)
        for c in range(3)
    ]


def fill_factors(coords, factor, slope=None):
    total = coords[0].shape[1]
    cells = lax.broadcasted_iota(jnp.int32, (SIDE, total), 0)
    for c in range(3):
        scaled = coords[c] * float(SIDE)
        floor_c = jnp.floor(scaled)
        fraction = scaled - floor_c
        weight = fraction * fraction * (3.0 - 2.0 * fraction)
        low = floor_c.astype(jnp.int32) & (SIDE - 1)
        high = (low + 1) & (SIDE - 1)
        low_hit = cells == low
        high_hit = cells == high
        factor[c] = jnp.where(low_hit, 1.0 - weight, jnp.where(high_hit, weight, 0.0))
        if slope is not None:
            change = float(SIDE) * 6.0 * fraction * (1.0 - fraction)
            slope[c] = jnp.where(low_hit, -change, jnp.where(high_hit, change, 0.0))


def block_place(lines):
    plane, block = pl.program_id(0), pl.program_id(1)
    return plane // 2, (plane + 3) // 2, block * lines


def fill_table(factor, table, lines):
    row_axis, col_axis, first = block_place(lines)

    def one(line, carry):
        row = factor[row_axis, pl.ds(first + line, 1), :]
        table[pl.ds(pl.multiple_of(line * SIDE, SIDE), SIDE), :] = (
            row * factor[col_axis]
        ).astype(BF16)
        return carry

    lax.fori_loop(0, lines, one, 0)


def network(features, first, hidden, heads):
    pre1 = dot(features, first)
    gate1 = jax.nn.sigmoid(pre1)
    hidden1 = (pre1 * gate1).astype(BF16)
    pre2 = dot(hidden1, hidden)
    gate2 = jax.nn.sigmoid(pre2)
    hidden2 = (pre2 * gate2).astype(BF16)
    last = dot(hidden2, heads)
    colors = jnp.tanh(last[:, :WIDTH])
    raw = last[:, WIDTH:]
    density = jnp.maximum(raw, 0.0) + jnp.log1p(jnp.exp(-jnp.abs(raw)))
    return pre1, gate1, hidden1, pre2, gate2, hidden2, colors, raw, density


def transmittance(density, samples):
    rows = density.shape[0] // samples
    depth = [density[s * rows : (s + 1) * rows] * STEP for s in range(samples)]
    before = jnp.zeros_like(depth[0])
    reach, kept = [], []
    for s in range(samples):
        reach.append(jnp.exp(-before))
        kept.append(jnp.exp(-depth[s]))
        before = before + depth[s]
    return reach, kept, jnp.exp(-before)


def last_step():
    return (pl.program_id(0) == pl.num_programs(0) - 1) & (
        pl.program_id(1) == pl.num_programs(1) - 1
    )


def first_step():
    return (pl.program_id(0) == 0) & (pl.program_id(1) == 0)


def forward_kernel(
    samples, lines, payload, planes, first, hidden, heads, message, features, factor, table, summed
):
    @pl.when(first_step())
    def _():
        fill_factors(coordinate_rows(payload[...], samples), factor)
        summed[...] = jnp.zeros_like(summed)

    fill_table(factor, table, lines)
    summed[...] += dot(planes[0].T.astype(BF16), table[...])

    @pl.when(last_step())
    def _():
        rounded = summed[...].T.astype(BF16)
        features[...] = rounded
        parts = network(rounded, first[...], hidden[...], heads[...])
        colors, density = parts[6], parts[8]
        reach, kept, passing = transmittance(density, samples)
        rows = passing.shape[0]
        value = jnp.zeros_like(passing)
        for s in range(samples):
            value = value + reach[s] * (1.0 - kept[s]) * colors[s * rows : (s + 1) * rows]
        message[:, :WIDTH] = value
        message[:, WIDTH:] = passing


def silu_slope(pre, gate):
    return gate * (1.0 + pre * (1.0 - gate))


def backward_kernel(
    samples,
    lines,
    payload,
    planes,
    first,
    hidden,
    heads,
    features,
    incoming,
    plane_grad,
    first_grad,
    hidden_grad,
    heads_grad,
    pose_grad,
    factor,
    slope,
    table,
    cot,
    point_grad,
):
    @pl.when(first_step())
    def _():
        fill_factors(coordinate_rows(payload[...], samples), factor, slope)
        point_grad[...] = jnp.zeros_like(point_grad)
        pre1, gate1, hidden1, pre2, gate2, hidden2, colors, raw, density = network(
            features[...], first[...], hidden[...], heads[...]
        )
        reach, kept, passing = transmittance(density, samples)
        rows = passing.shape[0]
        feature_cot = incoming[:, :WIDTH]
        pass_cot = incoming[:, WIDTH:] * passing
        behind = pass_cot
        color_cots = [None] * samples
        depth_cots = [None] * samples
        for s in reversed(range(samples)):
            here = colors[s * rows : (s + 1) * rows]
            along = jnp.sum(feature_cot * here, axis=1, keepdims=True)
            weight = reach[s] * (1.0 - kept[s])
            color_cots[s] = weight * feature_cot * (1.0 - here * here)
            depth_cots[s] = along * reach[s] * kept[s] - behind
            behind = behind + along * weight
        raw_cot = jnp.concatenate(depth_cots, axis=0) * STEP * jax.nn.sigmoid(raw)
        lane = lax.broadcasted_iota(jnp.int32, raw_cot.shape, 1)
        raw_cot = jnp.where(lane == 0, raw_cot, 0.0)
        last_cot = jnp.concatenate([jnp.concatenate(color_cots, axis=0), raw_cot], axis=1)
        last_cot = last_cot.astype(BF16)
        heads_grad[...] = dot(hidden2, last_cot, 0, 0).astype(BF16).astype(F32)
        cot2 = dot(last_cot, heads[...], 1, 1).astype(BF16).astype(F32)
        cot2 = (cot2 * silu_slope(pre2, gate2)).astype(BF16)
        hidden_grad[...] = dot(hidden1, cot2, 0, 0).astype(BF16).astype(F32)
        cot1 = dot(cot2, hidden[...], 1, 1).astype(BF16).astype(F32)
        cot1 = (cot1 * silu_slope(pre1, gate1)).astype(BF16)
        first_grad[...] = dot(features[...], cot1, 0, 0).astype(BF16).astype(F32)
        cot[...] = dot(cot1, first[...], 1, 1).astype(BF16)

    fill_table(factor, table, lines)
    plane_grad[0] = dot(table[...], cot[...])
    row_axis, col_axis, first_line = block_place(lines)
    total = cot.shape[0]

    def one(line, carry):
        cells = planes[0, pl.ds(pl.multiple_of(line * SIDE, SIDE), SIDE), :].astype(BF16)
        product = dot(cells, cot[...], 1, 1)
        by_col = (product * factor[col_axis]).reshape(SIDE // 8, 8, total).sum(0)
        by_slope = (product * slope[col_axis]).reshape(SIDE // 8, 8, total).sum(0)
        row = pl.ds(first_line + line, 1)
        point_grad[row_axis] += by_col * slope[row_axis, row, :]
        point_grad[col_axis] += by_slope * factor[row_axis, row, :]
        return carry

    lax.fori_loop(0, lines, one, 0)

    @pl.when(last_step())
    def _():
        columns = payload[...].T
        rows = columns.shape[1]
        base = 3 * samples
        anchor = [columns[base + c : base + c + 1] for c in range(3)]
        direction = [columns[base + 3 + c : base + 4 + c] for c in range(3)]
        place_grad, way_grad = [], []
        for c in range(3):
            whole = jnp.sum(point_grad[c], axis=0, keepdims=True)
            place = jnp.zeros((1, rows), F32)
            way = jnp.zeros((1, rows), F32)
            for s in range(samples):
                piece = whole[:, s * rows : (s + 1) * rows]
                place = place + piece
                way = way + piece * columns[base + 6 + s : base + 7 + s]
            place_grad.append(place)
            way_grad.append(way)
        turn = []
        for c in range(3):
            d, e = (c + 1) % 3, (c + 2) % 3
            turn.append(
                anchor[d] * place_grad[e]
                - anchor[e] * place_grad[d]
                + direction[d] * way_grad[e]
                - direction[e] * way_grad[d]
            )
        stacked = jnp.concatenate(turn + place_grad + [jnp.zeros((2, rows), F32)], axis=0)
        camera = payload[:, base + 6 + samples : base + 7 + samples]
        cameras = pose_grad.shape[1]
        named = lax.broadcasted_iota(jnp.int32, (rows, cameras), 1).astype(F32) == camera
        pose_grad[...] = exact_dot(stacked, named.astype(F32))


def cross_rows(left, right):
    return jnp.stack(
        [
            left[1] * right[2] - left[2] * right[1],
            left[2] * right[0] - left[0] * right[2],
            left[0] * right[1] - left[1] * right[0],
        ]
    )


def slot_numbers(target_brick, brick_count):
    onehot = (target_brick[:, None] == jnp.arange(brick_count)[None, :]).astype(F32)
    rows = target_brick.shape[0]
    lower = (jnp.arange(rows)[:, None] > jnp.arange(rows)[None, :]).astype(F32)
    before = jnp.dot(lower, onehot, preferred_element_type=F32)
    return jnp.sum(before * onehot, axis=1).astype(jnp.int32)


def whole_spec(shape):
    return pl.BlockSpec(shape, lambda *place: (0,) * len(shape))


def shaped(*shape):
    return jax.ShapeDtypeStruct(shape, F32)


def remote_params(number):
    return pltpu.CompilerParams(
        collective_id=number, has_side_effects=True, vmem_limit_bytes=VMEM_BYTES
    )


def per_device(
    anchors,
    directions,
    ray_start,
    camera_ids,
    brick_ids,
    brick_rank,
    targets,
    planes,
    first_weight,
    hidden_weight,
    feature_weight,
    density_weight,
    poses,
):
    count = lax.axis_size(AXES)
    ray_count, segs = brick_ids.shape
    samples = 4
    cap = 2 * ray_count * segs // count
    rows = -(-cap // 8) * 8
    listed = ray_count * segs
    slots = count * cap
    total = slots * samples
    cameras = poses.shape[1]
    in_vmem = pl.BlockSpec(memory_space=pltpu.VMEM)

    selector = (jnp.arange(cameras)[:, None] == camera_ids[None, :]).astype(F32)
    ray_pose = jnp.dot(poses, selector, precision=lax.Precision.HIGHEST)
    moved_anchor = anchors + cross_rows(ray_pose[0:3], anchors) + ray_pose[3:6]
    moved_direction = directions + cross_rows(ray_pose[0:3], directions)
    along = brick_rank.T.astype(F32)[:, :, None] * samples + jnp.arange(samples) + 0.5
    distance = ray_start[None, :, None] + along * STEP
    points = moved_anchor.T[None, :, :, None] + distance[:, :, None, :] * (
        moved_direction.T[None, :, :, None]
    )
    per_ray = jnp.concatenate([anchors.T, directions.T], axis=1)
    payload = jnp.concatenate(
        [
            points.reshape(listed, 3 * samples),
            jnp.tile(per_ray, (segs, 1)),
            distance.reshape(listed, samples),
            jnp.tile(camera_ids.astype(F32)[:, None], (segs, 1)),
        ],
        axis=1,
    )
    payload = jnp.pad(payload, ((0, 0), (0, WIDTH - payload.shape[1])))
    target_brick = brick_ids.T.reshape(-1)
    slot = target_brick * rows + slot_numbers(target_brick, count)
    slot_range = jnp.arange(count * rows)
    route = (slot[:, None] == slot_range[None, :]).astype(F32)
    route_back = (slot_range[:, None] == slot[None, :]).astype(F32)
    outgoing = jnp.dot(route_back, payload, precision=lax.Precision.HIGHEST)

    def narrow(padded):
        if rows == cap:
            return padded
        return padded.reshape(count, rows, -1)[:, :cap].reshape(slots, -1)

    def widen(packed):
        if rows == cap:
            return packed
        grouped = packed.reshape(count, cap, -1)
        return jnp.pad(grouped, ((0, 0), (0, rows - cap), (0, 0))).reshape(count * rows, -1)

    pair = [pltpu.SemaphoreType.DMA((count,)), pltpu.SemaphoreType.DMA((count,))]
    received = pl.pallas_call(
        functools.partial(points_kernel, count, rows),
        out_shape=shaped(count * rows, WIDTH),
        in_specs=[in_vmem],
        out_specs=in_vmem,
        scratch_shapes=[pltpu.VMEM((count * rows, WIDTH), F32)] + pair,
        compiler_params=remote_params(0),
        name="send_points",
    )(outgoing)
    received = narrow(received)

    first = first_weight[0].astype(BF16)
    hidden = hidden_weight[0, 0].astype(BF16)
    heads = jnp.concatenate(
        [feature_weight[0], jnp.broadcast_to(density_weight[0][:, None], feature_weight[0].shape)],
        axis=1,
    ).astype(BF16)
    channels = planes.shape[2]
    lines = 16
    cells = lines * SIDE
    grid = (3, SIDE // lines)
    plane_spec = pl.BlockSpec((1, cells, channels), lambda q, i: (0, q * (SIDE // lines) + i, 0))
    local = pltpu.CompilerParams(vmem_limit_bytes=VMEM_BYTES)
    message, features = pl.pallas_call(
        functools.partial(forward_kernel, samples, lines),
        grid=grid,
        out_shape=[shaped(slots, 2 * WIDTH), jax.ShapeDtypeStruct((total, channels), BF16)],
        in_specs=[whole_spec(received.shape), plane_spec]
        + [whole_spec(w.shape) for w in (first, hidden, heads)],
        out_specs=[whole_spec((slots, 2 * WIDTH)), whole_spec((total, channels))],
        scratch_shapes=[
            pltpu.VMEM((3, SIDE, total), F32),
            pltpu.VMEM((cells, total), BF16),
            pltpu.VMEM((channels, total), F32),
        ],
        compiler_params=local,
        name="brick_forward",
    )(received, planes, first, hidden, heads)

    wide = (count * rows, 2 * WIDTH)
    ray_feature, incoming = pl.pallas_call(
        functools.partial(owner_kernel, count, rows, ray_count, segs),
        out_shape=[shaped(ray_count, WIDTH), shaped(*wide)],
        in_specs=[in_vmem] * 5,
        out_specs=[in_vmem] * 2,
        scratch_shapes=[pltpu.VMEM(wide, F32)] * 3 + pair + pair,
        compiler_params=remote_params(1),
        name="rays",
    )(widen(message), route, route_back, brick_rank, targets)
    incoming = narrow(incoming)

    plane_grad, first_grad, hidden_grad, heads_grad, pose_local = pl.pallas_call(
        functools.partial(backward_kernel, samples, lines),
        grid=grid,
        out_shape=[
            jax.ShapeDtypeStruct(planes.shape, F32),
            shaped(*first.shape),
            shaped(*hidden.shape),
            shaped(*heads.shape),
            shaped(8, cameras),
        ],
        in_specs=[whole_spec(received.shape), plane_spec]
        + [whole_spec(w.shape) for w in (first, hidden, heads, features, incoming)],
        out_specs=[plane_spec]
        + [whole_spec(w.shape) for w in (first, hidden, heads)]
        + [whole_spec((8, cameras))],
        scratch_shapes=[
            pltpu.VMEM((3, SIDE, total), F32),
            pltpu.VMEM((3, SIDE, total), F32),
            pltpu.VMEM((cells, total), BF16),
            pltpu.VMEM((total, channels), BF16),
            pltpu.VMEM((3, 8, total), F32),
        ],
        compiler_params=local,
        name="brick_backward",
    )(received, planes, first, hidden, heads, features, incoming)

    pose_grad = pl.pallas_call(
        functools.partial(pose_kernel, count, 8),
        out_shape=shaped(8, cameras),
        in_specs=[in_vmem],
        out_specs=in_vmem,
        scratch_shapes=[pltpu.VMEM((count * 8, cameras), F32)] + pair,
        compiler_params=remote_params(2),
        name="sum_poses",
    )(pose_local)[:6]
    return (
        ray_feature,
        plane_grad,
        first_grad[None],
        hidden_grad[None, None],
        heads_grad[None, :, :WIDTH],
        heads_grad[None, :, WIDTH],
        pose_grad,
    )


def solution(mesh):
    split = P(AXES)
    in_specs = (P(None, AXES), P(None, AXES)) + (split,) * 10 + (P(),)
    out_specs = (split,) * 6 + (P(),)
    return jax.shard_map(
        per_device, mesh=mesh, in_specs=in_specs, out_specs=out_specs, check_vma=False
    )
```

time: 644 us -> 148 us (0.23)
  matrix products: 323 us -> 1.82 us
  Pallas kernels: 0 us -> 124 us
  other arithmetic: 83.6 us -> 12 us
  local copies, waits for them, and re-layouts: 69 us -> 8.38 us
  loops' own time: 57 us -> 0 us
  waiting for transfers between devices: 39.9 us -> 0 us
  blocking collectives: 38.4 us -> 0 us
  starting transfers between devices: 27.7 us -> 0 us
    dot_general x47 -> x3, matrix products: 323 us -> 1.82 us  [the longest x1 0.86 us: per_device(): outgoing = jnp.dot(route_back, payload, precision=lax.Precision.HIGHEST)]
    pallas_call x0 -> x5, Pallas kernels: none -> 124 us  [the longest x1 61 us: per_device(): pl.pallas_call(functools.partial(backward_kernel, samples, lines), grid=g...]
    another operation x3 -> x0, loops' own time: 57 us -> none  [lookup(): return lax.map(one_block, grouped).reshape(count, planes_flat.shape[1])]
    dynamic_update_slice x46 -> x0, local copies, waits for them, and re-layouts: 43.6 us -> none  [lookup(): return lax.map(one_block, grouped).reshape(count, planes_flat.shape[1])]
    all_to_all x6 -> x0, waiting for transfers between devices: 39.9 us -> none  [the longest x1 14.1 us: per_device(): lax.all_to_all(values_sent, ('gx', 'gy'), split_axis=0, concat_axis=0, ti...]
    psum x1 -> x0, blocking collectives: 38.4 us -> none  [per_device(): pose_grad = lax.psum(pose_local, ('gx', 'gy'))]
    mul x20 -> x1, other arithmetic: 38.7 us -> 0.69 us  [per_device(): brick_rank.T.astype(F32)[:, :, None] * samples + jnp.arange(samples) + 0.5]
    all_to_all x6 -> x0, starting transfers between devices: 27.7 us -> none  [the longest x1 7.3 us: per_device(): lax.all_to_all(outgoing, ('gx', 'gy'), split_axis=0, concat_axis=0, tiled...]
  transfers between devices with their start and end apart: 6 -> 0, of which waited for: 4 -> 0; matrix products, arithmetic and copies ran while one was open for 29% -> 0% of each run, Pallas kernels for 0% -> 0%
where the time goes in v1:
time: 148 us; the launch traced here: 147 us
  Pallas kernels  124 us (84%)
  other arithmetic  12 us (8%)
  local copies, waits for them, and re-layouts  8.38 us (6%)
  matrix products  1.82 us (1%)
    pallas_call x1, Pallas kernels, per_device(): pl.pallas_call(functools.partial(backward_kernel, samples, lines), grid=g...  61 us
    pallas_call x1, Pallas kernels, per_device(): pl.pallas_call(functools.partial(owner_kernel, count, rows, ray_count, se...  22.9 us
    pallas_call x1, Pallas kernels, per_device(): pl.pallas_call(functools.partial(forward_kernel, samples, lines), grid=gr...  14.8 us
    pallas_call x1, Pallas kernels, per_device(): pl.pallas_call(functools.partial(pose_kernel, count, 8), out_shape=shaped...  13 us
    pallas_call x1, Pallas kernels, per_device(): pl.pallas_call(functools.partial(points_kernel, count, rows), out_shape=s...  12.5 us
    unnamed x7, local copies, waits for them, and re-layouts  3.28 us

profile of v1, /device:TPU:0, one launch (start us, length us, event | category | flops | bytes accessed | tf_op | source)
XLA Modules:
  0.0 147.2 jit_solution(16864486094067252770)
XLA Ops:
  0.6 0.8 reshape.72
  1.4 0.2 fusion
  1.6 0.7 convert_reduce_fusion
  2.3 0.7 convert_element_type.52
  3.0 0.1 tile.20
  3.0 0.7 multiply_bitcast_fusion
  3.7 0.1 add.113
  3.8 0.7 add.110
  4.6 0.8 convolution_bitcast_fusion
  5.4 0.8 multiply_subtract_fusion.5
  6.3 0.8 multiply_subtract_fusion.2
  7.1 0.7 fusion.15
  7.8 0.7 pad_maximum_fusion.1
  8.5 0.7 multiply_add_fusion.1
  9.4 1.4 copy.25.ranks
  10.8 0.1 broadcast_in_dim.11
  10.9 1.5 %convert_bitcast_fusion.2.first = bf16[128,256]{1,0:T(8,128)(2,1)} fusion(f32[1,128,256]{2,1,0:T(8,128)} %param.21), kind=kLoop, calls=%fused_computation.23 | loop fusion | flops 32768 | bytes 196608 | tf_op jit(solution)/shard_map/convert_element_type | solution.py:518
  12.4 0.9 convert_bitcast_fusion.1
  13.3 0.7 pad_maximum_fusion.heads
  14.0 0.9 fusion.2.sent
  14.8 12.5 %send_points.1.payload = f32[256,128]{1,0:T(8,128)} custom-call(f32[256,128]{1,0:T(8,128)} %fusion.2.sent), custom_call_target="tpu_custom_call" | custom-call | tf_op jit(solution)/shard_map/send_points/pallas_call | solution.py:507
  27.4 1.6 %convert_bitcast_fusion.hidden = bf16[256,256]{1,0:T(8,128)(2,1)} fusion(f32[1,1,256,256]{3,2,1,0:T(8,128)} %param.22), kind=kLoop, calls=%fused_computation.7 | loop fusion | flops 65536 | bytes 393216 | tf_op jit(solution)/shard_map/convert_element_type | solution.py:519
  29.0 0.7 fusion.1.route_back
  29.7 0.7 fusion.3.route
  30.4 14.8 %brick_forward.1 = (f32[256,256]{1,0:T(8,128)}, bf16[1024,128]{1,0:T(8,128)(2,1)}) custom-call(f32[256,128]{1,0:T(8,128)} %send_points.1.payload, f32[1,12288,128]{2,1,0:T(8,128)} %planes.3, bf16[128,256]{1,0:T(8,128)(2,1)} %convert_bitcast_fusion.2.first, bf16[256,256]{1,0:T(8,128)(2,1)} %convert_bitcast_fusion.hidden, bf16[256,256]{1,0:T(8,128)(2,1)} %pad_maximum_fusion.heads), custom_call_target="tpu_custom_call" | custom-call | tf_op jit(solution)/shard_map/brick_forward/pallas_call | solution.py:530
  45.2 22.9 %rays.1 = (f32[32,128]{1,0:T(8,128)}, f32[256,256]{1,0:T(8,128)}) custom-call(f32[256,256]{1,0:T(8,128)} %get-tuple-element.16.sent, f32[128,256]{1,0:T(8,128)} %fusion.3.route, f32[256,128]{1,0:T(8,128)} %fusion.1.route_back, s32[32,4]{1,0:T(8,128)} %copy.25.ranks, f32[32,128]{1,0:T(8,128)} %targets.1), custom_call_target="tpu_custom_call" | custom-call | tf_op jit(solution)/shard_map/rays/pallas_call | solution.py:547
  68.2 61.0 %brick_backward.1 = (f32[1,12288,128]{2,1,0:T(8,128)}, f32[128,256]{1,0:T(8,128)}, f32[256,256]{1,0:T(8,128)}, f32[256,256]{1,0:T(8,128)}, f32[8,256]{1,0:T(8,128)}) custom-call(f32[256,128]{1,0:T(8,128)} %send_points.1.payload, f32[1,12288,128]{2,1,0:T(8,128)} %planes.3, bf16[128,256]{1,0:T(8,128)(2,1)} %convert_bitcast_fusion.2.first, ...), custom_call_target="tpu_custom_call" | custom-call | tf_op jit(solution)/shard_map/brick_backward/pallas_call | solution.py:558
  129.1 1.6 %slice_reduce_fusion = f32[256]{0:T(256)} fusion(f32[256,256]{1,0:T(8,128)} %get-tuple-element.23), kind=kLoop, calls=%fused_computation.4 | loop fusion | bytes 2048 | tf_op jit(solution)/shard_map/slice | solution.py:599
  130.7 1.6 %slice_bitcast_fusion = f32[1,256,128]{2,1,0:T(8,128)} fusion(f32[256,256]{1,0:T(8,128)} %get-tuple-element.23), kind=kLoop, calls=%fused_computation.5 | loop fusion | bytes 262144 | tf_op jit(solution)/shard_map/broadcast_in_dim | solution.py:598
  132.3 13.0 %sum_poses.1 = f32[8,256]{1,0:T(8,128)} custom-call(f32[8,256]{1,0:T(8,128)} %get-tuple-element.24.own), custom_call_target="tpu_custom_call" | custom-call | tf_op jit(solution)/shard_map/sum_poses/pallas_call | solution.py:584
  145.3 0.6 copy.28
  145.9 1.3 copy.29
  (13 shorter events, 0.4 us)
Async XLA Ops:
  0.6 4.0 %copy-start = (f32[6,256]{1,0:T(8,128)S(1)}, f32[6,256]{1,0:T(8,128)}, u32[]{:S(2)}) copy-start(f32[6,256]{1,0:T(8,128)} %param.25) | copy-start | bytes 18436
  68.2 77.1 %copy-start.1 = (f32[32,128]{1,0:T(8,128)S(1)}, f32[32,128]{1,0:T(8,128)}, u32[]{:S(2)}) copy-start(f32[32,128]{1,0:T(8,128)} %get-tuple-element.40) | copy-start | bytes 49156

commit v2 on v1

--- a/solution.py
+++ b/solution.py
@@ -51,7 +51,10 @@
         return carry
 
     lax.fori_loop(1, count, greet, 0)
-    pl.semaphore_wait(barrier, count - 1)
+
+
+def all_entered(count):
+    pl.semaphore_wait(pltpu.get_barrier_semaphore(), count - 1)
 
 
 def rows_of(ref, index, rows):
@@ -108,8 +111,52 @@
     target[here, :] = source[here, :]
 
 
-def points_kernel(count, rows, sent, received, landed, send_sem, recv_sem):
+def cross_rows(left, right):
+    return [
+        left[1] * right[2] - left[2] * right[1],
+        left[2] * right[0] - left[0] * right[2],
+        left[0] * right[1] - left[1] * right[0],
+    ]
+
+
+def row_list(array, start, number):
+    return [array[start + c : start + c + 1] for c in range(number)]
+
+
+def points_kernel(
+    count, rows, samples, listing, poses, received, route_out, sent, landed, send_sem, recv_sem
+):
     enter(count)
+    listed = listing.shape[1]
+    anchors = row_list(listing, 0, 3)
+    directions = row_list(listing, 3, 3)
+    ray_start, camera, rank, brick = row_list(listing, 6, 4)
+    cameras = lax.broadcasted_iota(jnp.int32, (poses.shape[1], listed), 0).astype(F32)
+    ray_pose = exact_dot(poses[...], (cameras == camera).astype(F32))
+    turned_anchor = cross_rows(row_list(ray_pose, 0, 3), anchors)
+    turned_direction = cross_rows(row_list(ray_pose, 0, 3), directions)
+    moved_anchor = [anchors[c] + turned_anchor[c] + ray_pose[3 + c : 4 + c] for c in range(3)]
+    moved_direction = [directions[c] + turned_direction[c] for c in range(3)]
+    distance = [ray_start + (rank * samples + s + 0.5) * STEP for s in range(samples)]
+    payload = [
+        moved_anchor[c] + distance[s] * moved_direction[c]
+        for c in range(3)
+        for s in range(samples)
+    ]
+    payload = payload + anchors + directions + distance + [camera]
+    filler = jnp.zeros((WIDTH - len(payload), listed), F32)
+    payload = jnp.concatenate(payload + [filler], axis=0)
+    bricks = lax.broadcasted_iota(jnp.int32, (count, listed), 0).astype(F32)
+    named = (bricks == brick).astype(F32)
+    earlier = lax.broadcasted_iota(jnp.int32, (listed, listed), 0)
+    later = lax.broadcasted_iota(jnp.int32, (listed, listed), 1)
+    before = dot(named.astype(BF16), (earlier < later).astype(BF16))
+    slot = brick * rows + jnp.sum(before * named, axis=0, keepdims=True)
+    slots = lax.broadcasted_iota(jnp.int32, (count * rows, listed), 0).astype(F32)
+    route = (slots == slot).astype(F32)
+    route_out[...] = route
+    sent[...] = exact_dot(route, payload, 1, 1)
+    all_entered(count)
     send_all(count, sent, landed, rows, send_sem, recv_sem)
     keep_own(sent, landed, rows)
     wait_all(count, sent, landed, rows, send_sem, recv_sem)
@@ -123,7 +170,6 @@
     segs,
     sent,
     route,
-    route_back,
     ranks,
     targets,
     ray_out,
@@ -137,10 +183,11 @@
     recv_sem2,
 ):
     enter(count)
+    all_entered(count)
     send_all(count, sent, home, rows, send_sem, recv_sem)
     keep_own(sent, home, rows)
     wait_all(count, sent, home, rows, send_sem, recv_sem)
-    listed = exact_dot(route[...], home[...])
+    listed = exact_dot(route[...], home[...], 0, 0)
     feature = [listed[k * ray_count : (k + 1) * ray_count, :WIDTH] for k in range(segs)]
     passing = [listed[k * ray_count : (k + 1) * ray_count, WIDTH:] for k in range(segs)]
     rank = [
@@ -171,7 +218,7 @@
                     rank[k] < rank[behind], through(behind, k) * along[behind], 0.0
                 )
         back.append(jnp.concatenate([transmit[k] * residual, pass_grad], axis=1))
-    outgoing[...] = exact_dot(route_back[...], jnp.concatenate(back, axis=0))
+    outgoing[...] = exact_dot(route[...], jnp.concatenate(back, axis=0))
     send_all(count, outgoing, landed, rows, send_sem2, recv_sem2)
     keep_own(outgoing, landed, rows)
     wait_all(count, outgoing, landed, rows, send_sem2, recv_sem2)
@@ -180,6 +227,7 @@
 
 def pose_kernel(count, rows, own, total, landed, send_sem, recv_sem):
     enter(count)
+    all_entered(count)
     send_all(count, own, landed, rows, send_sem, recv_sem, shared=True)
     here = pl.ds(pl.multiple_of(my_index() * rows, 8), rows)
     landed[here, :] = own[...]
@@ -187,7 +235,7 @@
     summed = landed[0:rows, :]
     for index in range(1, count):
         summed = summed + landed[index * rows : (index + 1) * rows, :]
-    total[...] = summed
+    total[...] = summed[: total.shape[0]]
 
 
 def coordinate_rows(payload, samples):
@@ -234,6 +282,12 @@
     lax.fori_loop(0, lines, one, 0)
 
 
+def bf16_weights(first, hidden, feature, density):
+    column = jnp.broadcast_to(density[...], (WIDTH, density.shape[1])).T
+    heads = jnp.concatenate([feature[0], column], axis=1).astype(BF16)
+    return first[0].astype(BF16), hidden[0, 0].astype(BF16), heads
+
+
 def network(features, first, hidden, heads):
     pre1 = dot(features, first)
     gate1 = jax.nn.sigmoid(pre1)
@@ -271,7 +325,19 @@
 
 
 def forward_kernel(
-    samples, lines, payload, planes, first, hidden, heads, message, features, factor, table, summed
+    samples,
+    lines,
+    payload,
+    planes,
+    first,
+    hidden,
+    feature,
+    density,
+    message,
+    features,
+    factor,
+    table,
+    summed,
 ):
     @pl.when(first_step())
     def _():
@@ -285,9 +351,9 @@
     def _():
         rounded = summed[...].T.astype(BF16)
         features[...] = rounded
-        parts = network(rounded, first[...], hidden[...], heads[...])
-        colors, density = parts[6], parts[8]
-        reach, kept, passing = transmittance(density, samples)
+        parts = network(rounded, *bf16_weights(first, hidden, feature, density))
+        colors = parts[6]
+        reach, kept, passing = transmittance(parts[8], samples)
         rows = passing.shape[0]
         value = jnp.zeros_like(passing)
         for s in range(samples):
@@ -307,28 +373,33 @@
     planes,
     first,
     hidden,
-    heads,
+    feature,
+    density,
     features,
     incoming,
     plane_grad,
     first_grad,
     hidden_grad,
-    heads_grad,
+    feature_grad,
+    density_grad,
     pose_grad,
     factor,
     slope,
     table,
     cot,
+    cot_rows,
+    product,
     point_grad,
 ):
     @pl.when(first_step())
     def _():
         fill_factors(coordinate_rows(payload[...], samples), factor, slope)
         point_grad[...] = jnp.zeros_like(point_grad)
-        pre1, gate1, hidden1, pre2, gate2, hidden2, colors, raw, density = network(
-            features[...], first[...], hidden[...], heads[...]
+        weight1, weight2, heads = bf16_weights(first, hidden, feature, density)
+        pre1, gate1, hidden1, pre2, gate2, hidden2, colors, raw, thick = network(
+            features[...], weight1, weight2, heads
         )
-        reach, kept, passing = transmittance(density, samples)
+        reach, kept, passing = transmittance(thick, samples)
         rows = passing.shape[0]
         feature_cot = incoming[:, :WIDTH]
         pass_cot = incoming[:, WIDTH:] * passing
@@ -347,31 +418,42 @@
         raw_cot = jnp.where(lane == 0, raw_cot, 0.0)
         last_cot = jnp.concatenate([jnp.concatenate(color_cots, axis=0), raw_cot], axis=1)
         last_cot = last_cot.astype(BF16)
-        heads_grad[...] = dot(hidden2, last_cot, 0, 0).astype(BF16).astype(F32)
-        cot2 = dot(last_cot, heads[...], 1, 1).astype(BF16).astype(F32)
+        feature_grad[0] = dot(hidden2, last_cot[:, :WIDTH], 0, 0).astype(BF16).astype(F32)
+        by_density = dot(last_cot[:, WIDTH:], hidden2, 0, 0)
+        density_grad[...] = by_density[0:1].astype(BF16).astype(F32)
+        cot2 = dot(last_cot, heads, 1, 1).astype(BF16).astype(F32)
         cot2 = (cot2 * silu_slope(pre2, gate2)).astype(BF16)
-        hidden_grad[...] = dot(hidden1, cot2, 0, 0).astype(BF16).astype(F32)
-        cot1 = dot(cot2, hidden[...], 1, 1).astype(BF16).astype(F32)
+        hidden_grad[0, 0] = dot(hidden1, cot2, 0, 0).astype(BF16).astype(F32)
+        cot1 = dot(cot2, weight2, 1, 1).astype(BF16).astype(F32)
         cot1 = (cot1 * silu_slope(pre1, gate1)).astype(BF16)
-        first_grad[...] = dot(features[...], cot1, 0, 0).astype(BF16).astype(F32)
-        cot[...] = dot(cot1, first[...], 1, 1).astype(BF16)
+        first_grad[0] = dot(features[...], cot1, 0, 0).astype(BF16).astype(F32)
+        sample_cot = dot(cot1, weight1, 1, 1)
+        cot[...] = sample_cot.astype(BF16)
+        cot_rows[...] = sample_cot.T.astype(BF16)
 
     fill_table(factor, table, lines)
     plane_grad[0] = dot(table[...], cot[...])
     row_axis, col_axis, first_line = block_place(lines)
-    total = cot.shape[0]
-
-    def one(line, carry):
-        cells = planes[0, pl.ds(pl.multiple_of(line * SIDE, SIDE), SIDE), :].astype(BF16)
-        product = dot(cells, cot[...], 1, 1)
-        by_col = (product * factor[col_axis]).reshape(SIDE // 8, 8, total).sum(0)
-        by_slope = (product * slope[col_axis]).reshape(SIDE // 8, 8, total).sum(0)
-        row = pl.ds(first_line + line, 1)
-        point_grad[row_axis] += by_col * slope[row_axis, row, :]
-        point_grad[col_axis] += by_slope * factor[row_axis, row, :]
+    product[...] = dot(planes[0].astype(BF16), cot_rows[...])
+
+    def one(chunk, carry):
+        lanes = pl.ds(pl.multiple_of(chunk * WIDTH, WIDTH), WIDTH)
+        col, col_slope = factor[col_axis, :, lanes], slope[col_axis, :, lanes]
+        here = pl.ds(pl.multiple_of(first_line, 8), lines)
+        rows, row_slopes = factor[row_axis, here, lanes], slope[row_axis, here, lanes]
+        row_total = jnp.zeros((8, WIDTH), F32)
+        col_total = jnp.zeros((8, WIDTH), F32)
+        for line in range(lines):
+            piece = product[line * SIDE : (line + 1) * SIDE, lanes]
+            by_col = (piece * col).reshape(SIDE // 8, 8, WIDTH).sum(0)
+            by_slope = (piece * col_slope).reshape(SIDE // 8, 8, WIDTH).sum(0)
+            row_total = row_total + by_col * row_slopes[line : line + 1]
+            col_total = col_total + by_slope * rows[line : line + 1]
+        point_grad[row_axis, :, lanes] += row_total
+        point_grad[col_axis, :, lanes] += col_total
         return carry
 
-    lax.fori_loop(0, lines, one, 0)
+    lax.fori_loop(0, cot.shape[0] // WIDTH, one, 0)
 
     @pl.when(last_step())
     def _():
@@ -407,24 +489,6 @@
         pose_grad[...] = exact_dot(stacked, named.astype(F32))
 
 
-def cross_rows(left, right):
-    return jnp.stack(
-        [
-            left[1] * right[2] - left[2] * right[1],
-            left[2] * right[0] - left[0] * right[2],
-            left[0] * right[1] - left[1] * right[0],
-        ]
-    )
-
-
-def slot_numbers(target_brick, brick_count):
-    onehot = (target_brick[:, None] == jnp.arange(brick_count)[None, :]).astype(F32)
-    rows = target_brick.shape[0]
-    lower = (jnp.arange(rows)[:, None] > jnp.arange(rows)[None, :]).astype(F32)
-    before = jnp.dot(lower, onehot, preferred_element_type=F32)
-    return jnp.sum(before * onehot, axis=1).astype(jnp.int32)
-
-
 def whole_spec(shape):
     return pl.BlockSpec(shape, lambda *place: (0,) * len(shape))
 
@@ -465,32 +529,17 @@
     cameras = poses.shape[1]
     in_vmem = pl.BlockSpec(memory_space=pltpu.VMEM)
 
-    selector = (jnp.arange(cameras)[:, None] == camera_ids[None, :]).astype(F32)
-    ray_pose = jnp.dot(poses, selector, precision=lax.Precision.HIGHEST)
-    moved_anchor = anchors + cross_rows(ray_pose[0:3], anchors) + ray_pose[3:6]
-    moved_direction = directions + cross_rows(ray_pose[0:3], directions)
-    along = brick_rank.T.astype(F32)[:, :, None] * samples + jnp.arange(samples) + 0.5
-    distance = ray_start[None, :, None] + along * STEP
-    points = moved_anchor.T[None, :, :, None] + distance[:, :, None, :] * (
-        moved_direction.T[None, :, :, None]
+    per_ray = jnp.concatenate(
+        [anchors, directions, ray_start[None], camera_ids.astype(F32)[None]], axis=0
     )
-    per_ray = jnp.concatenate([anchors.T, directions.T], axis=1)
-    payload = jnp.concatenate(
+    listing = jnp.concatenate(
         [
-            points.reshape(listed, 3 * samples),
-            jnp.tile(per_ray, (segs, 1)),
-            distance.reshape(listed, samples),
-            jnp.tile(camera_ids.astype(F32)[:, None], (segs, 1)),
+            jnp.tile(per_ray, (1, segs)),
+            brick_rank.T.reshape(1, listed).astype(F32),
+            brick_ids.T.reshape(1, listed).astype(F32),
         ],
-        axis=1,
+        axis=0,
     )
-    payload = jnp.pad(payload, ((0, 0), (0, WIDTH - payload.shape[1])))
-    target_brick = brick_ids.T.reshape(-1)
-    slot = target_brick * rows + slot_numbers(target_brick, count)
-    slot_range = jnp.arange(count * rows)
-    route = (slot[:, None] == slot_range[None, :]).astype(F32)
-    route_back = (slot_range[:, None] == slot[None, :]).astype(F32)
-    outgoing = jnp.dot(route_back, payload, precision=lax.Precision.HIGHEST)
 
     def narrow(padded):
         if rows == cap:
@@ -504,23 +553,18 @@
         return jnp.pad(grouped, ((0, 0), (0, rows - cap), (0, 0))).reshape(count * rows, -1)
 
     pair = [pltpu.SemaphoreType.DMA((count,)), pltpu.SemaphoreType.DMA((count,))]
-    received = pl.pallas_call(
-        functools.partial(points_kernel, count, rows),
-        out_shape=shaped(count * rows, WIDTH),
-        in_specs=[in_vmem],
-        out_specs=in_vmem,
-        scratch_shapes=[pltpu.VMEM((count * rows, WIDTH), F32)] + pair,
+    received, route = pl.pallas_call(
+        functools.partial(points_kernel, count, rows, samples),
+        out_shape=[shaped(count * rows, WIDTH), shaped(count * rows, listed)],
+        in_specs=[in_vmem] * 2,
+        out_specs=[in_vmem] * 2,
+        scratch_shapes=[pltpu.VMEM((count * rows, WIDTH), F32)] * 2 + pair,
         compiler_params=remote_params(0),
         name="send_points",
-    )(outgoing)
+    )(listing, poses)
     received = narrow(received)
 
-    first = first_weight[0].astype(BF16)
-    hidden = hidden_weight[0, 0].astype(BF16)
-    heads = jnp.concatenate(
-        [feature_weight[0], jnp.broadcast_to(density_weight[0][:, None], feature_weight[0].shape)],
-        axis=1,
-    ).astype(BF16)
+    weights = (first_weight, hidden_weight, feature_weight, density_weight)
     channels = planes.shape[2]
     lines = 16
     cells = lines * SIDE
@@ -532,7 +576,7 @@
         grid=grid,
         out_shape=[shaped(slots, 2 * WIDTH), jax.ShapeDtypeStruct((total, channels), BF16)],
         in_specs=[whole_spec(received.shape), plane_spec]
-        + [whole_spec(w.shape) for w in (first, hidden, heads)],
+        + [whole_spec(w.shape) for w in weights],
         out_specs=[whole_spec((slots, 2 * WIDTH)), whole_spec((total, channels))],
         scratch_shapes=[
             pltpu.VMEM((3, SIDE, total), F32),
@@ -541,64 +585,56 @@
         ],
         compiler_params=local,
         name="brick_forward",
-    )(received, planes, first, hidden, heads)
+    )(received, planes, *weights)
 
     wide = (count * rows, 2 * WIDTH)
     ray_feature, incoming = pl.pallas_call(
         functools.partial(owner_kernel, count, rows, ray_count, segs),
         out_shape=[shaped(ray_count, WIDTH), shaped(*wide)],
-        in_specs=[in_vmem] * 5,
+        in_specs=[in_vmem] * 4,
         out_specs=[in_vmem] * 2,
         scratch_shapes=[pltpu.VMEM(wide, F32)] * 3 + pair + pair,
         compiler_params=remote_params(1),
         name="rays",
-    )(widen(message), route, route_back, brick_rank, targets)
+    )(widen(message), route, brick_rank, targets)
     incoming = narrow(incoming)
 
-    plane_grad, first_grad, hidden_grad, heads_grad, pose_local = pl.pallas_call(
+    plane_grad, *weight_grads, pose_local = pl.pallas_call(
         functools.partial(backward_kernel, samples, lines),
         grid=grid,
         out_shape=[
-            jax.ShapeDtypeStruct(planes.shape, F32),
-            shaped(*first.shape),
-            shaped(*hidden.shape),
-            shaped(*heads.shape),
+            shaped(*planes.shape),
+            *(shaped(*w.shape) for w in weights),
             shaped(8, cameras),
         ],
         in_specs=[whole_spec(received.shape), plane_spec]
-        + [whole_spec(w.shape) for w in (first, hidden, heads, features, incoming)],
+        + [whole_spec(w.shape) for w in weights + (features, incoming)],
         out_specs=[plane_spec]
-        + [whole_spec(w.shape) for w in (first, hidden, heads)]
+        + [whole_spec(w.shape) for w in weights]
         + [whole_spec((8, cameras))],
         scratch_shapes=[
             pltpu.VMEM((3, SIDE, total), F32),
             pltpu.VMEM((3, SIDE, total), F32),
             pltpu.VMEM((cells, total), BF16),
             pltpu.VMEM((total, channels), BF16),
+            pltpu.VMEM((channels, total), BF16),
+            pltpu.VMEM((cells, total), F32),
             pltpu.VMEM((3, 8, total), F32),
         ],
         compiler_params=local,
         name="brick_backward",
-    )(received, planes, first, hidden, heads, features, incoming)
+    )(received, planes, *weights, features, incoming)
 
     pose_grad = pl.pallas_call(
         functools.partial(pose_kernel, count, 8),
-        out_shape=shaped(8, cameras),
+        out_shape=shaped(*poses.shape),
         in_specs=[in_vmem],
         out_specs=in_vmem,
         scratch_shapes=[pltpu.VMEM((count * 8, cameras), F32)] + pair,
         compiler_params=remote_params(2),
         name="sum_poses",
-    )(pose_local)[:6]
-    return (
-        ray_feature,
-        plane_grad,
-        first_grad[None],
-        hidden_grad[None, None],
-        heads_grad[None, :, :WIDTH],
-        heads_grad[None, :, WIDTH],
-        pose_grad,
-    )
+    )(pose_local)
+    return (ray_feature, plane_grad, *weight_grads, pose_grad)
 
 
 def solution(mesh):

time: 148 us -> 107 us (0.72)
  Pallas kernels: 124 us -> 99.1 us
  other arithmetic: 12 us -> 3.36 us
  local copies, waits for them, and re-layouts: 8.38 us -> 3.53 us
  matrix products: 1.82 us -> 0 us
    pallas_call x1, Pallas kernels: 61 us -> 35.9 us  [per_device(): pl.pallas_call(functools.partial(backward_kernel, samples, lines), grid=g...]
    convert_element_type x6 -> x2, other arithmetic: 5.22 us -> 1.37 us  [the longest x1 0.68 us: per_device(): brick_rank.T.reshape(1, listed).astype(F32)]
    dot_general x3 -> x0, matrix products: 1.82 us -> none  [the longest x1 0.86 us: per_device(): outgoing = jnp.dot(route_back, payload, precision=lax.Precision.HIGHEST)]
    broadcast_in_dim x2 -> x0, local copies, waits for them, and re-layouts: 1.66 us -> none  [the longest x1 1.57 us: per_device(): heads_grad[None, :, :WIDTH]]
    sub x2 -> x0, other arithmetic: 1.61 us -> none  [cross_rows(): left[1] * right[2] - left[2] * right[1]]
    slice x1 -> x0, local copies, waits for them, and re-layouts: 1.58 us -> none  [per_device(): heads_grad[None, :, WIDTH]]
    unnamed x7 -> x5, local copies, waits for them, and re-layouts: 3.28 us -> 3.27 us
where the time goes in v2:
time: 107 us
  Pallas kernels  99.1 us (93%)
  local copies, waits for them, and re-layouts  3.53 us (3%)
  other arithmetic  3.36 us (3%)
    pallas_call x1, Pallas kernels, per_device(): pl.pallas_call(functools.partial(backward_kernel, samples, lines), grid=g...  35.9 us
    pallas_call x1, Pallas kernels, per_device(): pl.pallas_call(functools.partial(owner_kernel, count, rows, ray_count, se...  22.9 us
    pallas_call x1, Pallas kernels, per_device(): pl.pallas_call(functools.partial(forward_kernel, samples, lines), grid=gr...  14.9 us
    pallas_call x1, Pallas kernels, per_device(): pl.pallas_call(functools.partial(pose_kernel, count, 8), out_shape=shaped...  13 us
    pallas_call x1, Pallas kernels, per_device(): pl.pallas_call(functools.partial(points_kernel, count, rows, samples), ou...  12.4 us
    unnamed x5, local copies, waits for them, and re-layouts  3.27 us

profile of v2, /device:TPU:0, one launch (start us, length us, event | category | flops | bytes accessed | tf_op | source)
XLA Modules:
  0.0 106.7 jit_solution(13167991327731434893)
XLA Ops:
  0.6 0.7 convert_bitcast_fusion.2
  1.3 0.7 convert_bitcast_fusion
  2.0 0.1 convert_element_type.43
  2.1 0.7 convert_bitcast_fusion.1
  2.7 0.1 convert_element_type.40
  2.8 0.7 pad_maximum_fusion.1
  3.6 0.1 tile.10
  3.6 0.6 pad_maximum_fusion.listing
  4.3 1.4 %copy.20.ranks = s32[32,4]{1,0:T(8,128)} copy(s32[32,4]{0,1:T(4,128)} %param.18) | data formatting | bytes 1024 | tf_op args[5]
  5.6 12.4 %send_points.1 = (f32[256,128]{1,0:T(8,128)}, f32[256,128]{1,0:T(8,128)}) custom-call(f32[10,128]{1,0:T(8,128)} %pad_maximum_fusion.listing, f32[6,256]{1,0:T(8,128)} %poses.1), custom_call_target="tpu_custom_call" | custom-call | tf_op jit(solution)/shard_map/send_points/pallas_call | solution.py:556
  18.1 14.9 %brick_forward.1 = (f32[256,256]{1,0:T(8,128)}, bf16[1024,128]{1,0:T(8,128)(2,1)}) custom-call(f32[256,128]{1,0:T(8,128)} %get-tuple-element.19.payload, f32[1,12288,128]{2,1,0:T(8,128)} %planes.3, f32[1,128,256]{2,1,0:T(8,128)} %first.3, f32[1,1,256,256]{3,2,1,0:T(8,128)} %hidden.3, f32[1,256,128]{2,1,0:T(8,128)} %feature.3, f32[1,256]{1,0:T(1,128)} %density.3), custom_call_target="tpu_custom_call" | custom-call | tf_op jit(solution)/shard_map/brick_forward/pallas_call | solution.py:574
  33.0 22.9 %rays.1 = (f32[32,128]{1,0:T(8,128)}, f32[256,256]{1,0:T(8,128)}) custom-call(f32[256,256]{1,0:T(8,128)} %get-tuple-element.20.sent, f32[256,128]{1,0:T(8,128)} %get-tuple-element.21.route, s32[32,4]{1,0:T(8,128)} %copy.20.ranks, f32[32,128]{1,0:T(8,128)} %targets.1), custom_call_target="tpu_custom_call" | custom-call | tf_op jit(solution)/shard_map/rays/pallas_call | solution.py:591
  55.9 0.0 copy-start
  55.9 35.9 %brick_backward.1 = (f32[1,12288,128]{2,1,0:T(8,128)}, f32[1,128,256]{2,1,0:T(8,128)}, f32[1,1,256,256]{3,2,1,0:T(8,128)}, f32[1,256,128]{2,1,0:T(8,128)}, f32[1,256]{1,0:T(1,128)}, /*index=5*/f32[8,256]{1,0:T(8,128)}) custom-call(f32[256,128]{1,0:T(8,128)} %get-tuple-element.19.payload, f32[1,12288,128]{2,1,0:T(8,128)} %planes.3, f32[1,128,256]{2,1,0:T(8,128)} %first.3, ...), custom_call_target="tpu_custom_call" | custom-call | tf_op jit(solution)/shard_map/brick_backward/pallas_call | solution.py:602
  91.7 13.0 %sum_poses.1 = f32[6,256]{1,0:T(8,128)} custom-call(f32[8,256]{1,0:T(8,128)} %get-tuple-element.30.own), custom_call_target="tpu_custom_call" | custom-call | tf_op jit(solution)/shard_map/sum_poses/pallas_call | solution.py:628
  104.8 0.0 copy-done
  104.8 0.6 copy.23
  105.4 1.3 %copy.24 = f32[6,256]{1,0:T(8,128)} copy(f32[6,256]{1,0:T(8,128)} %sum_poses.1) | data formatting | bytes 12288
  (1 shorter events, 0.0 us)
Async XLA Ops:
  55.9 48.9 %copy-start = (f32[32,128]{1,0:T(8,128)S(1)}, f32[32,128]{1,0:T(8,128)}, u32[]{:S(2)}) copy-start(f32[32,128]{1,0:T(8,128)} %get-tuple-element.38) | copy-start | bytes 49156

commit v3 on v2

--- a/solution.py
+++ b/solution.py
@@ -61,11 +61,11 @@
     return ref.at[pl.ds(pl.multiple_of(index * rows, 8), rows)]
 
 
-def remote_copy(count, step, source, target, rows, send_sem, recv_sem, shared):
+def remote_copy(count, step, source, target, rows, send_sem, recv_sem):
     me = my_index()
     peer = (me + step) % count
     return pltpu.make_async_remote_copy(
-        src_ref=source if shared else rows_of(source, peer, rows),
+        src_ref=rows_of(source, peer, rows),
         dst_ref=rows_of(target, me, rows),
         send_sem=send_sem.at[step],
         recv_sem=recv_sem.at[me],
@@ -74,21 +74,21 @@
     )
 
 
-def send_all(count, source, target, rows, send_sem, recv_sem, shared=False):
+def send_all(count, source, target, rows, send_sem, recv_sem):
     def send(step, carry):
-        remote_copy(count, step, source, target, rows, send_sem, recv_sem, shared).start()
+        remote_copy(count, step, source, target, rows, send_sem, recv_sem).start()
         return carry
 
     lax.fori_loop(1, count, send, 0)
 
 
-def wait_all(count, source, target, rows, send_sem, recv_sem, shared=False):
+def wait_all(count, source, target, rows, send_sem, recv_sem):
     me = my_index()
 
     def arrive(step, carry):
         origin = (me + count - step) % count
         pltpu.make_async_remote_copy(
-            src_ref=source if shared else rows_of(source, origin, rows),
+            src_ref=rows_of(source, origin, rows),
             dst_ref=rows_of(target, origin, rows),
             send_sem=send_sem.at[step],
             recv_sem=recv_sem.at[origin],
@@ -100,7 +100,7 @@
     lax.fori_loop(1, count, arrive, 0)
 
     def leave(step, carry):
-        remote_copy(count, step, source, target, rows, send_sem, recv_sem, shared).wait_send()
+        remote_copy(count, step, source, target, rows, send_sem, recv_sem).wait_send()
         return carry
 
     lax.fori_loop(1, count, leave, 0)
@@ -170,7 +170,7 @@
     segs,
     sent,
     route,
-    ranks,
+    listing,
     targets,
     ray_out,
     received,
@@ -190,10 +190,8 @@
     listed = exact_dot(route[...], home[...], 0, 0)
     feature = [listed[k * ray_count : (k + 1) * ray_count, :WIDTH] for k in range(segs)]
     passing = [listed[k * ray_count : (k + 1) * ray_count, WIDTH:] for k in range(segs)]
-    rank = [
-        jnp.broadcast_to(ranks[:, k : k + 1], (ray_count, WIDTH)).astype(F32)
-        for k in range(segs)
-    ]
+    ranks = jnp.broadcast_to(listing[8:9, :], (WIDTH, segs * ray_count)).T
+    rank = [ranks[k * ray_count : (k + 1) * ray_count] for k in range(segs)]
 
     def through(k, skipped):
         product = jnp.ones((ray_count, WIDTH), F32)
@@ -225,16 +223,55 @@
     received[...] = landed[...]
 
 
-def pose_kernel(count, rows, own, total, landed, send_sem, recv_sem):
-    enter(count)
-    all_entered(count)
-    send_all(count, own, landed, rows, send_sem, recv_sem, shared=True)
-    here = pl.ds(pl.multiple_of(my_index() * rows, 8), rows)
-    landed[here, :] = own[...]
-    wait_all(count, own, landed, rows, send_sem, recv_sem, shared=True)
+def along_axis(axis, index):
+    place = {name: lax.axis_index(name) for name in AXES}
+    place[axis] = index
+    return tuple(place[name] for name in AXES)
+
+
+def share_along(axis, rows, own, landed, send_sem, recv_sem):
+    count, me = lax.axis_size(axis), lax.axis_index(axis)
+
+    def copy(step, target, index):
+        return pltpu.make_async_remote_copy(
+            src_ref=own,
+            dst_ref=rows_of(landed, index, rows),
+            send_sem=send_sem.at[step],
+            recv_sem=recv_sem.at[index],
+            device_id=along_axis(axis, target),
+            device_id_type=MESH_ID,
+        )
+
+    for step in range(1, count):
+        copy(step, (me + step) % count, me).start()
+    landed[pl.ds(pl.multiple_of(me * rows, 8), rows), :] = own[...]
+    for step in range(1, count):
+        origin = (me + count - step) % count
+        copy(step, origin, origin).wait_recv()
+    for step in range(1, count):
+        copy(step, (me + step) % count, me).wait_send()
     summed = landed[0:rows, :]
     for index in range(1, count):
         summed = summed + landed[index * rows : (index + 1) * rows, :]
+    return summed
+
+
+def pose_kernel(rows, own, total, near, part, far, near_send, near_recv, far_send, far_recv):
+    barrier = pltpu.get_barrier_semaphore()
+    greeted = 0
+    for axis in AXES:
+        count = lax.axis_size(axis)
+        for step in range(1, count):
+            pl.semaphore_signal(
+                barrier,
+                inc=1,
+                device_id=along_axis(axis, (lax.axis_index(axis) + step) % count),
+                device_id_type=MESH_ID,
+            )
+        greeted += count - 1
+    pl.semaphore_wait(barrier, greeted)
+    part[...] = share_along("gy", rows, own, near, near_send, near_recv)
+    summed = share_along("gx", rows, part, far, far_send, far_recv)
     total[...] = summed[: total.shape[0]]
 
 
@@ -271,15 +308,11 @@
 
 def fill_table(factor, table, lines):
     row_axis, col_axis, first = block_place(lines)
-
-    def one(line, carry):
-        row = factor[row_axis, pl.ds(first + line, 1), :]
-        table[pl.ds(pl.multiple_of(line * SIDE, SIDE), SIDE), :] = (
-            row * factor[col_axis]
+    rows = factor[row_axis, pl.ds(pl.multiple_of(first, 8), lines), :]
+    for line in range(lines):
+        table[line * SIDE : (line + 1) * SIDE, :] = (
+            rows[line : line + 1] * factor[col_axis]
         ).astype(BF16)
-        return carry
-
-    lax.fori_loop(0, lines, one, 0)
 
 
 def bf16_weights(first, hidden, feature, density):
@@ -431,10 +464,10 @@
         cot[...] = sample_cot.astype(BF16)
         cot_rows[...] = sample_cot.T.astype(BF16)
 
+    product[...] = dot(planes[0].astype(BF16), cot_rows[...])
     fill_table(factor, table, lines)
     plane_grad[0] = dot(table[...], cot[...])
     row_axis, col_axis, first_line = block_place(lines)
-    product[...] = dot(planes[0].astype(BF16), cot_rows[...])
 
     def one(chunk, carry):
         lanes = pl.ds(pl.multiple_of(chunk * WIDTH, WIDTH), WIDTH)
@@ -453,7 +486,7 @@
         point_grad[col_axis, :, lanes] += col_total
         return carry
 
-    lax.fori_loop(0, cot.shape[0] // WIDTH, one, 0)
+    lax.fori_loop(0, cot.shape[0] // WIDTH, one, 0, unroll=True)
 
     @pl.when(last_step())
     def _():
@@ -596,7 +629,7 @@
         scratch_shapes=[pltpu.VMEM(wide, F32)] * 3 + pair + pair,
         compiler_params=remote_params(1),
         name="rays",
-    )(widen(message), route, brick_rank, targets)
+    )(widen(message), route, listing, targets)
     incoming = narrow(incoming)
 
     plane_grad, *weight_grads, pose_local = pl.pallas_call(
@@ -625,12 +658,19 @@
         name="brick_backward",
     )(received, planes, *weights, features, incoming)
 
+    far, near = (lax.axis_size(axis) for axis in AXES)
     pose_grad = pl.pallas_call(
-        functools.partial(pose_kernel, count, 8),
+        functools.partial(pose_kernel, 8),
         out_shape=shaped(*poses.shape),
         in_specs=[in_vmem],
         out_specs=in_vmem,
-        scratch_shapes=[pltpu.VMEM((count * 8, cameras), F32)] + pair,
+        scratch_shapes=[
+            pltpu.VMEM((8 * near, cameras), F32),
+            pltpu.VMEM((8, cameras), F32),
+            pltpu.VMEM((8 * far, cameras), F32),
+        ]
+        + [pltpu.SemaphoreType.DMA((near,))] * 2
+        + [pltpu.SemaphoreType.DMA((far,))] * 2,
         compiler_params=remote_params(2),
         name="sum_poses",
     )(pose_local)

time: 107 us -> 89.3 us (0.83)
  Pallas kernels: 99.1 us -> 82.5 us
  local copies, waits for them, and re-layouts: 3.53 us -> 2.17 us
    pallas_call x1, Pallas kernels: 35.9 us -> 22.3 us  [per_device(): pl.pallas_call(functools.partial(backward_kernel, samples, lines), grid=g...]
    pallas_call x1, Pallas kernels: 14.9 us -> 12.7 us  [per_device(): pl.pallas_call(functools.partial(forward_kernel, samples, lines), grid=gr...]
    unnamed x5 -> x4, local copies, waits for them, and re-layouts: 3.27 us -> 1.91 us
where the time goes in v3:
time: 89.3 us; the launch traced here: 88.7 us
  Pallas kernels  82.5 us (92%)
  other arithmetic  3.36 us (4%)
  local copies, waits for them, and re-layouts  2.17 us (2%)
    pallas_call x1, Pallas kernels, per_device(): pl.pallas_call(functools.partial(owner_kernel, count, rows, ray_count, se...  22.9 us
    pallas_call x1, Pallas kernels, per_device(): pl.pallas_call(functools.partial(backward_kernel, samples, lines), grid=g...  22.3 us
    pallas_call x1, Pallas kernels, per_device(): pl.pallas_call(functools.partial(forward_kernel, samples, lines), grid=gr...  12.7 us
    pallas_call x1, Pallas kernels, per_device(): pl.pallas_call(functools.partial(points_kernel, count, rows, samples), ou...  12.4 us
    pallas_call x1, Pallas kernels, per_device(): pl.pallas_call(functools.partial(pose_kernel, 8), out_shape=shaped(*poses...  12.2 us
    unnamed x4, local copies, waits for them, and re-layouts  1.91 us

profile of v3, /device:TPU:0, one launch (start us, length us, event | category | flops | bytes accessed | tf_op | source)
XLA Modules:
  0.0 88.7 jit_solution(7369799606627020773)
XLA Ops:
  0.6 0.7 convert_bitcast_fusion.2
  1.3 0.7 convert_bitcast_fusion
  2.0 0.1 convert_element_type.43
  2.1 0.7 convert_bitcast_fusion.1
  2.7 0.1 convert_element_type.40
  2.8 0.7 pad_maximum_fusion.1
  3.6 0.1 tile.10
  3.6 0.6 pad_maximum_fusion.listing
  4.3 12.4 %send_points.1 = (f32[256,128]{1,0:T(8,128)}, f32[256,128]{1,0:T(8,128)}) custom-call(f32[10,128]{1,0:T(8,128)} %pad_maximum_fusion.listing, f32[6,256]{1,0:T(8,128)} %poses.1), custom_call_target="tpu_custom_call" | custom-call | tf_op jit(solution)/shard_map/send_points/pallas_call | solution.py:589
  16.7 12.7 %brick_forward.1 = (f32[256,256]{1,0:T(8,128)}, bf16[1024,128]{1,0:T(8,128)(2,1)}) custom-call(f32[256,128]{1,0:T(8,128)} %get-tuple-element.19.payload, f32[1,12288,128]{2,1,0:T(8,128)} %planes.3, f32[1,128,256]{2,1,0:T(8,128)} %first.3, f32[1,1,256,256]{3,2,1,0:T(8,128)} %hidden.3, f32[1,256,128]{2,1,0:T(8,128)} %feature.3, f32[1,256]{1,0:T(1,128)} %density.3), custom_call_target="tpu_custom_call" | custom-call | tf_op jit(solution)/shard_map/brick_forward/pallas_call | solution.py:607
  29.4 22.9 %rays.1 = (f32[32,128]{1,0:T(8,128)}, f32[256,256]{1,0:T(8,128)}) custom-call(f32[256,256]{1,0:T(8,128)} %get-tuple-element.20.sent, f32[256,128]{1,0:T(8,128)} %get-tuple-element.21.route, f32[10,128]{1,0:T(8,128)} %pad_maximum_fusion.listing, f32[32,128]{1,0:T(8,128)} %targets.1), custom_call_target="tpu_custom_call" | custom-call | tf_op jit(solution)/shard_map/rays/pallas_call | solution.py:624
  52.3 0.0 copy-start
  52.3 22.3 %brick_backward.1 = (f32[1,12288,128]{2,1,0:T(8,128)}, f32[1,128,256]{2,1,0:T(8,128)}, f32[1,1,256,256]{3,2,1,0:T(8,128)}, f32[1,256,128]{2,1,0:T(8,128)}, f32[1,256]{1,0:T(1,128)}, /*index=5*/f32[8,256]{1,0:T(8,128)}) custom-call(f32[256,128]{1,0:T(8,128)} %get-tuple-element.19.payload, f32[1,12288,128]{2,1,0:T(8,128)} %planes.3, f32[1,128,256]{2,1,0:T(8,128)} %first.3, ...), custom_call_target="tpu_custom_call" | custom-call | tf_op jit(solution)/shard_map/brick_backward/pallas_call | solution.py:635
  74.6 12.2 %sum_poses.1 = f32[6,256]{1,0:T(8,128)} custom-call(f32[8,256]{1,0:T(8,128)} %get-tuple-element.30.own), custom_call_target="tpu_custom_call" | custom-call | tf_op jit(solution)/shard_map/sum_poses/pallas_call | solution.py:662
  86.8 0.0 copy-done
  86.8 0.6 copy.22
  87.4 1.3 %copy.23 = f32[6,256]{1,0:T(8,128)} copy(f32[6,256]{1,0:T(8,128)} %sum_poses.1) | data formatting | bytes 12288
  (1 shorter events, 0.0 us)
Async XLA Ops:
  52.3 34.5 %copy-start = (f32[32,128]{1,0:T(8,128)S(1)}, f32[32,128]{1,0:T(8,128)}, u32[]{:S(2)}) copy-start(f32[32,128]{1,0:T(8,128)} %get-tuple-element.38) | copy-start | bytes 49156

commit v4 on v3

--- a/solution.py
+++ b/solution.py
@@ -181,8 +181,10 @@
     recv_sem,
     send_sem2,
     recv_sem2,
+    greeted=False,
 ):
-    enter(count)
+    if not greeted:
+        enter(count)
     all_entered(count)
     send_all(count, sent, home, rows, send_sem, recv_sem)
     keep_own(sent, home, rows)
@@ -393,6 +395,24 @@
             value = value + reach[s] * (1.0 - kept[s]) * colors[s * rows : (s + 1) * rows]
         message[:, :WIDTH] = value
         message[:, WIDTH:] = passing
+
+
+def forward_rays_kernel(count, rows, ray_count, segs, samples, lines, *refs):
+    local_in, owner_in = refs[:6], refs[6:9]
+    features, ray_out, received = refs[9:12]
+    message, factor, table, summed = refs[12:16]
+
+    @pl.when(first_step())
+    def _():
+        enter(count)
+
+    forward_kernel(samples, lines, *local_in, message, features, factor, table, summed)
+
+    @pl.when(last_step())
+    def _():
+        owner_kernel(
+            count, rows, ray_count, segs, message, *owner_in, ray_out, received, *refs[16:], greeted=True
+        )
 
 
 def silu_slope(pre, gate):
@@ -604,32 +624,63 @@
     grid = (3, SIDE // lines)
     plane_spec = pl.BlockSpec((1, cells, channels), lambda q, i: (0, q * (SIDE // lines) + i, 0))
     local = pltpu.CompilerParams(vmem_limit_bytes=VMEM_BYTES)
-    message, features = pl.pallas_call(
-        functools.partial(forward_kernel, samples, lines),
-        grid=grid,
-        out_shape=[shaped(slots, 2 * WIDTH), jax.ShapeDtypeStruct((total, channels), BF16)],
-        in_specs=[whole_spec(received.shape), plane_spec]
-        + [whole_spec(w.shape) for w in weights],
-        out_specs=[whole_spec((slots, 2 * WIDTH)), whole_spec((total, channels))],
-        scratch_shapes=[
-            pltpu.VMEM((3, SIDE, total), F32),
-            pltpu.VMEM((cells, total), BF16),
-            pltpu.VMEM((channels, total), F32),
-        ],
-        compiler_params=local,
-        name="brick_forward",
-    )(received, planes, *weights)
-
     wide = (count * rows, 2 * WIDTH)
-    ray_feature, incoming = pl.pallas_call(
-        functools.partial(owner_kernel, count, rows, ray_count, segs),
-        out_shape=[shaped(ray_count, WIDTH), shaped(*wide)],
-        in_specs=[in_vmem] * 4,
-        out_specs=[in_vmem] * 2,
-        scratch_shapes=[pltpu.VMEM(wide, F32)] * 3 + pair + pair,
-        compiler_params=remote_params(1),
-        name="rays",
-    )(widen(message), route, listing, targets)
+    lookup_scratch = [
+        pltpu.VMEM((3, SIDE, total), F32),
+        pltpu.VMEM((cells, total), BF16),
+        pltpu.VMEM((channels, total), F32),
+    ]
+    if rows == cap:
+        owner_in = (route, listing, targets)
+        features, ray_feature, incoming = pl.pallas_call(
+            functools.partial(forward_rays_kernel, count, rows, ray_count, segs, samples, lines),
+            grid=grid,
+            out_shape=[
+                jax.ShapeDtypeStruct((total, channels), BF16),
+                shaped(ray_count, WIDTH),
+                shaped(*wide),
+            ],
+            in_specs=[whole_spec(received.shape), plane_spec]
+            + [whole_spec(w.shape) for w in weights + owner_in],
+            out_specs=[
+                whole_spec((total, channels)),
+                whole_spec((ray_count, WIDTH)),
+                whole_spec(wide),
+            ],
+            scratch_shapes=[pltpu.VMEM(wide, F32)]
+            + lookup_scratch
+            + [pltpu.VMEM(wide, F32)] * 3
+            + pair
+            + pair,
+            compiler_params=remote_params(1),
+            name="brick_forward_rays",
+        )(received, planes, *weights, *owner_in)
+    else:
+        message, features = pl.pallas_call(
+            functools.partial(forward_kernel, samples, lines),
+            grid=grid,
+            out_shape=[shaped(slots, 2 * WIDTH), jax.ShapeDtypeStruct((total, channels), BF16)],
+            in_specs=[whole_spec(received.shape), plane_spec]
+            + [whole_spec(w.shape) for w in weights],
+            out_specs=[whole_spec((slots, 2 * WIDTH)), whole_spec((total, channels))],
+            scratch_shapes=[
+                pltpu.VMEM((3, SIDE, total), F32),
+                pltpu.VMEM((cells, total), BF16),
+                pltpu.VMEM((channels, total), F32),
+            ],
+            compiler_params=local,
+            name="brick_forward",
+        )(received, planes, *weights)
+
+        ray_feature, incoming = pl.pallas_call(
+            functools.partial(owner_kernel, count, rows, ray_count, segs),
+            out_shape=[shaped(ray_count, WIDTH), shaped(*wide)],
+            in_specs=[in_vmem] * 4,
+            out_specs=[in_vmem] * 2,
+            scratch_shapes=[pltpu.VMEM(wide, F32)] * 3 + pair + pair,
+            compiler_params=remote_params(1),
+            name="rays",
+        )(widen(message), route, listing, targets)
     incoming = narrow(incoming)
 
     plane_grad, *weight_grads, pose_local = pl.pallas_call(

time: 89.3 us -> 85.7 us (0.960)
  Pallas kernels: 82.5 us -> 79 us
    pallas_call x2 -> x1, Pallas kernels: 35.6 us -> 30.8 us  [per_device(): pl.pallas_call(functools.partial(forward_rays_kernel, count, rows, ray_co...]
    pallas_call x1, Pallas kernels: 12.2 us -> 13.5 us  [per_device(): pl.pallas_call(functools.partial(pose_kernel, 8), out_shape=shaped(*poses...]
where the time goes in v4:
time: 85.7 us; the launch traced here: 85.2 us
  Pallas kernels  79 us (92%)
  other arithmetic  3.36 us (4%)
  local copies, waits for them, and re-layouts  2.17 us (3%)
    pallas_call x1, Pallas kernels, per_device(): pl.pallas_call(functools.partial(forward_rays_kernel, count, rows, ray_co...  30.8 us
    pallas_call x1, Pallas kernels, per_device(): pl.pallas_call(functools.partial(backward_kernel, samples, lines), grid=g...  22.3 us
    pallas_call x1, Pallas kernels, per_device(): pl.pallas_call(functools.partial(pose_kernel, 8), out_shape=shaped(*poses...  13.5 us
    pallas_call x1, Pallas kernels, per_device(): pl.pallas_call(functools.partial(points_kernel, count, rows, samples), ou...  12.4 us
    unnamed x4, local copies, waits for them, and re-layouts  1.91 us

profile of v4, /device:TPU:0, one launch (start us, length us, event | category | flops | bytes accessed | tf_op | source)
XLA Modules:
  0.0 85.2 jit_solution(13359179659118752445)
XLA Ops:
  0.6 0.7 convert_bitcast_fusion.2
  1.3 0.7 convert_bitcast_fusion
  2.0 0.1 convert_element_type.43
  2.1 0.7 convert_bitcast_fusion.1
  2.7 0.1 convert_element_type.40
  2.8 0.7 pad_maximum_fusion.1
  3.6 0.1 tile.10
  3.6 0.6 pad_maximum_fusion.listing.refs_7_
  4.3 12.4 %send_points.1 = (f32[256,128]{1,0:T(8,128)}, f32[256,128]{1,0:T(8,128)}) custom-call(f32[10,128]{1,0:T(8,128)} %pad_maximum_fusion.listing.refs_7_, f32[6,256]{1,0:T(8,128)} %poses.1), custom_call_target="tpu_custom_call" | custom-call | tf_op jit(solution)/shard_map/send_points/pallas_call | solution.py:609
  16.7 30.8 %brick_forward_rays.1 = (bf16[1024,128]{1,0:T(8,128)(2,1)}, f32[32,128]{1,0:T(8,128)}, f32[256,256]{1,0:T(8,128)}) custom-call(f32[256,128]{1,0:T(8,128)} %get-tuple-element.18.refs_0_.payload, f32[1,12288,128]{2,1,0:T(8,128)} %planes.1, f32[1,128,256]{2,1,0:T(8,128)} %first.1, f32[1,1,256,256]{3,2,1,0:T(8,128)} %hidden.1, f32[1,256,128]{2,1,0:T(8,128)} %feature.1, ...), custom_call_target="tpu_custom_call" | custom-call | tf_op jit(solution)/shard_map/brick_forward_rays/pallas_call | solution.py:635
  47.5 0.0 copy-start
  47.5 22.3 %brick_backward.1 = (f32[1,12288,128]{2,1,0:T(8,128)}, f32[1,128,256]{2,1,0:T(8,128)}, f32[1,1,256,256]{3,2,1,0:T(8,128)}, f32[1,256,128]{2,1,0:T(8,128)}, f32[1,256]{1,0:T(1,128)}, /*index=5*/f32[8,256]{1,0:T(8,128)}) custom-call(f32[256,128]{1,0:T(8,128)} %get-tuple-element.18.refs_0_.payload, f32[1,12288,128]{2,1,0:T(8,128)} %planes.1, ...), custom_call_target="tpu_custom_call" | custom-call | tf_op jit(solution)/shard_map/brick_backward/pallas_call | solution.py:686
  69.8 13.5 %sum_poses.1 = f32[6,256]{1,0:T(8,128)} custom-call(f32[8,256]{1,0:T(8,128)} %get-tuple-element.28.own), custom_call_target="tpu_custom_call" | custom-call | tf_op jit(solution)/shard_map/sum_poses/pallas_call | solution.py:713
  83.3 0.0 copy-done
  83.3 0.6 copy.22
  83.9 1.3 %copy.23 = f32[6,256]{1,0:T(8,128)} copy(f32[6,256]{1,0:T(8,128)} %sum_poses.1) | data formatting | bytes 12288
  (1 shorter events, 0.0 us)
Async XLA Ops:
  47.5 35.8 %copy-start = (f32[32,128]{1,0:T(8,128)S(1)}, f32[32,128]{1,0:T(8,128)}, u32[]{:S(2)}) copy-start(f32[32,128]{1,0:T(8,128)} %get-tuple-element.36) | copy-start | bytes 49156
